TPU v7x, 32 devices: a whole 2x2x4 slice. The times are simulated.
32 devices in a mesh: comp: 4 (over z), tile: 8 (over y, x, core).
Axes of the slice: x: 2, y: 2, z: 4, core: 2. Of those that a mesh axis runs over, the one named last changes fastest.
Arguments:
- vertical_profile_fields: float32 [192, 65536], P(None, ('comp', 'tile')), may hold values from -6 to 6
- implicit_diffusion_solver: float32 [192, 192], replicated, may hold values from -0.4375 to 0.4375
- prior_seawater_warmth: float32 [65536], P(('comp', 'tile')), may hold values from -6 to 6
- overlay_share_matrices: float32 [32, 256, 512], P('comp'), may hold values from 0.0009765625 to 0.015625
- overlay_pairings: int32 [3, 2048], P(None, ('comp', 'tile')), may hold values from 0 to 255, as said below
- marine_top_fields: float32 [4, 128, 4096], P(None, 'comp', 'tile'), may hold values from -6 to 6
- marine_indicator: int32 [128, 4096], P('comp', 'tile'), may hold values 0 or 1
Outputs:
- atm_new: float32 [192, 65536], P(None, ('comp', 'tile'))
- marine_fields_stepped: float32 [4, 128, 4096], P(None, 'comp', 'tile')
- seawater_warmth_regridded: float32 [65536], P(('comp', 'tile'))
Inputs may be any that keep to these rules, and one draw needn't show every extreme that they name: `overlay_pairings`: row 0: on the device at comp c, tile t each id is j * 8 + t with j < 8, and each of its 8 blocks is named at least once. Row 1: ids of ocean blocks of the same band, q * 32 + r for row r of the ocean tile of tile index q; each device names every ocean tile either 0 or exactly 16 times, and in every band one ocean tile is named 16 times by every device of the band. Row 2: weight block indices below 8.
All inputs are finite; a program needn't handle non-finite values. No bound on the sum of `marine_indicator` on one device may be relied on, other than what follows from the above.
Results may differ from a plain program's by a relative error of at most 0.0003.
Values sent between devices are 32-bit elements; how exact they have to be, the bound alone decides.
A program may use at most 64 MiB of HBM per device.

v0:
```python
import jax
import jax.numpy as jnp
from jax import lax
from jax.sharding import PartitionSpec as P

VERTICAL_LAYERS = 48
F = 4
BA = 256
ABLK = 8
OVL_DEV = 64
WTAB = 8
OX = 32
SUB = 20


precise = lax.Precision.HIGHEST
wave_speed = 0.25
mixing = 0.15
rotation = 0.1
tracer_mixing = 0.2
forcing_rate = 0.05
transfer_constant = 0.5
dewpoint_moisture_limit = 0.6


def padded_2(shard, sides, width):
    for axis, dim in sides:
        size, length = (lax.axis_size(axis), shard.shape[dim])
        up = [(i, (i + 1) % size) for i in range(size - 1)]
        down = [(j, i) for i, j in up]
        last = lax.slice_in_dim(shard, length - width, length, axis=dim)
        first = lax.slice_in_dim(shard, 0, width, axis=dim)
        before = lax.ppermute(last, axis, up)
        after = lax.ppermute(first, axis, down)
        shard = jnp.concatenate([before, shard, after], axis=dim)
    return shard


def vertical_mixing_step(vertical_profile_fields, implicit_diffusion_solver, prior_seawater_warmth):
    renewed_profile_fields = jnp.dot(
        implicit_diffusion_solver,
        vertical_profile_fields,
        precision=precise,
        preferred_element_type=jnp.float32,
    )
    lower_troposphere_warmth = renewed_profile_fields[VERTICAL_LAYERS - 1]
    moisture_content = renewed_profile_fields[2 * VERTICAL_LAYERS - 1]
    wind_east = renewed_profile_fields[3 * VERTICAL_LAYERS - 1]
    wind_north = renewed_profile_fields[4 * VERTICAL_LAYERS - 1]
    breeze_speed = jnp.sqrt(wind_east * wind_east + wind_north * wind_north + 1.0)
    conductive_energy_transfer = (
        transfer_constant * breeze_speed * (prior_seawater_warmth - lower_troposphere_warmth)
    )
    evaporation_rate = (
        transfer_constant
        * breeze_speed
        * (dewpoint_moisture_limit * prior_seawater_warmth - moisture_content)
    )
    stress_east = transfer_constant * breeze_speed * wind_east
    stress_north = transfer_constant * breeze_speed * wind_north
    return (
        renewed_profile_fields,
        jnp.stack([conductive_energy_transfer, evaporation_rate, stress_east, stress_north]),
    )


def advance(padded, sea_mask, forcing):
    centre = padded[:, 1:-1, 1:-1]
    north_cells = padded[:, 2:, 1:-1]
    south_cells = padded[:, :-2, 1:-1]
    east_cells = padded[:, 1:-1, 2:]
    west_cells = padded[:, 1:-1, :-2]
    laplace = north_cells + south_cells + east_cells + west_cells - 4.0 * centre
    along_east = 0.5 * (east_cells - west_cells)
    along_north = 0.5 * (north_cells - south_cells)
    height = (
        centre[0]
        - wave_speed * (along_east[1] + along_north[2])
        + mixing * laplace[0]
        + forcing_rate * forcing[1]
    )
    zonal_flow = (
        centre[1]
        - wave_speed * along_east[0]
        + rotation * centre[2]
        + mixing * laplace[1]
        + forcing_rate * forcing[2]
    )
    meridional_flow = (
        centre[2]
        - wave_speed * along_north[0]
        - rotation * centre[1]
        + mixing * laplace[2]
        + forcing_rate * forcing[3]
    )
    surface = centre[3] + tracer_mixing * laplace[3] + forcing_rate * forcing[0]
    return jnp.stack([height, zonal_flow, meridional_flow, surface]) * sea_mask


def body(
    vertical_profile_fields,
    implicit_diffusion_solver,
    prior_seawater_warmth,
    overlay_share_matrices,
    overlay_pairings,
    marine_top_fields,
    marine_indicator,
):
    renewed_profile_fields, interface_transfers = vertical_mixing_step(
        vertical_profile_fields, implicit_diffusion_solver, prior_seawater_warmth
    )
    blocks = interface_transfers.reshape(F, ABLK, BA).transpose(1, 0, 2)
    tile_count = lax.axis_size("tile")
    capacity = max(2, 2 * OVL_DEV // tile_count)
    own_tile = lax.axis_index("tile")
    air_block = overlay_pairings[0] // tile_count
    ocean_tile = overlay_pairings[1] // OX
    table_index = overlay_pairings[2]
    slot_order = jnp.arange(OVL_DEV)
    earlier = (ocean_tile[:, None] == ocean_tile[None, :]) & (
        slot_order[None, :] < slot_order[:, None]
    )
    position = jnp.sum(earlier.astype(jnp.int32), axis=1)
    sea_mask = marine_indicator.astype(jnp.float32)
    band_flux, zonal_strip_members = (
        lax.all_gather(blocks, "tile", axis=0, tiled=True),
        lax.all_gather(overlay_pairings.astype(jnp.float32), "tile", axis=1, tiled=True),
    )
    listing = zonal_strip_members.astype(jnp.int32)
    source = jnp.arange(tile_count * OVL_DEV) // OVL_DEV
    block_index = source * ABLK + listing[0] // tile_count
    aimed_here = listing[1] // OX == own_tile
    target_row = listing[1] % OX
    group_code = jnp.where(aimed_here, target_row * WTAB + listing[2], OX * WTAB)
    counts = (
        jnp.zeros((OX * WTAB, tile_count * ABLK), jnp.float32)
        .at[group_code, block_index]
        .add(1.0, mode="drop")
    )
    grouped = jnp.dot(
        counts,
        band_flux.reshape(tile_count * ABLK, F * BA),
        precision=precise,
        preferred_element_type=jnp.float32,
    )
    forcing = jnp.einsum(
        "rwfa,wao->fro", grouped.reshape(OX, WTAB, F, BA), overlay_share_matrices, precision=precise
    )
    aimed_grid = aimed_here.reshape(tile_count, OVL_DEV).astype(jnp.int32)
    slot_place = jnp.cumsum(aimed_grid, axis=1) - aimed_grid
    slot_place = jnp.where(aimed_grid > 0, slot_place, capacity)
    sender = jnp.broadcast_to(jnp.arange(tile_count)[:, None], (tile_count, OVL_DEV))
    return_rows = (
        jnp.zeros((tile_count, capacity), jnp.int32)
        .at[sender, slot_place]
        .set(target_row.reshape(tile_count, OVL_DEV), mode="drop")
    )

    def substep(substep_index, fields):
        padded = padded_2(fields, (("comp", 1), ("tile", 2)), 1)
        return advance(padded, sea_mask, forcing)

    marine_fields_stepped = lax.fori_loop(0, SUB, substep, marine_top_fields)
    outgoing_surface = marine_fields_stepped[3][return_rows]
    arrived = lax.all_to_all(outgoing_surface, "tile", split_axis=0, concat_axis=0, tiled=True)
    surface_rows = arrived[ocean_tile, position]
    combos_back = jnp.einsum("ko,wao->kwa", surface_rows, overlay_share_matrices, precision=precise)
    chosen = combos_back[slot_order, table_index]
    weight_sums = jnp.sum(overlay_share_matrices, axis=2)[table_index]
    numerator = jnp.zeros((ABLK, BA), jnp.float32).at[air_block].add(chosen)
    denominator = jnp.zeros((ABLK, BA), jnp.float32).at[air_block].add(weight_sums)
    return (renewed_profile_fields, marine_fields_stepped, (numerator / denominator).reshape(-1))


def solution(mesh):
    placed = (
        P(None, ("comp", "tile")),
        P(),
        P(("comp", "tile")),
        P("comp", None, None),
        P(None, ("comp", "tile")),
        P(None, "comp", "tile"),
        P("comp", "tile"),
    )
    return jax.shard_map(
        body,
        mesh=mesh,
        in_specs=placed,
        out_specs=(P(None, ("comp", "tile")), P(None, "comp", "tile"), P(("comp", "tile"))),
        check_vma=False,
    )
```

profile of v0, /device:TPU:0, one launch (start us, length us, event | category | flops | bytes accessed | tf_op | source)
XLA Modules:
  0.0 437.7 jit_solution(5258825029313480163)
XLA Ops:
  0.6 1.4 copy-done
  2.0 2.4 fusion.75
  5.7 10.8 %all_gather.7 = f32[64,4,256]{2,1,0:T(4,128)S(1)} all-gather(f32[8,4,256]{2,1,0:T(4,128)S(1)} %maximum_bitcast_fusion), channel_id=1, replica_groups=mesh['comp'=4,'tile'=8] {'tile'}, dimensions={0}, use_global_device_ids=true | all-gather | bytes 294912 | tf_op jit(solution)/shard_map/all_gather | solution.py:126
  16.7 8.9 %all-gather = f32[8,64,3]{1,2,0:T(4,128)S(1)} all-gather(f32[1,64,3]{1,2,0:T(4,128)S(1)} %convert_bitcast_fusion), channel_id=1, replica_groups=mesh['comp'=4,'tile'=8] {'tile'}, dimensions={0}, use_global_device_ids=true | all-gather | bytes 6912 | tf_op jit(solution)/shard_map/all_gather | solution.py:127
  25.7 25.9 %scatter_fusion = f32[256,64]{0,1:T(8,128)S(1)} fusion(f32[256,64]{0,1:T(8,128)S(1)} %broadcast_in_dim.16, s32[512]{0:T(512)S(1)} %bitcast.125, f32[512]{0:T(512)S(1)} %broadcast.675), kind=kCustom, calls=%fused_computation.4 | custom fusion | flops 512 | bytes 10240 | tf_op jit(solution)/shard_map/scatter-add | solution.py:138
  52.8 4.7 %fusion.16 = f32[4,32,512]{2,1,0:T(8,128)S(1)} fusion(f32[32,8,4,256]{3,0,1,2:T(8,128)S(1)} %fusion.26, f32[8,256,512]{2,1,0:T(8,128)} %param.12), kind=kOutput, calls=%fused_computation.46 | convolution fusion | flops 1610612736 | bytes 5505024 | tf_op jit(solution)/shard_map/rwfa,wao->fro/dot_general | solution.py:146
  57.5 323.6 %while.10 = (s32[]{:T(128)}, f32[4,32,512]{2,1,0:T(8,128)S(1)}, f32[4,32,512]{2,1,0:T(8,128)S(1)}, f32[32,512]{1,0:T(8,128)S(1)}, s32[]{:T(128)}) while((s32[]{:T(128)}, f32[4,32,512]{2,1,0:T(8,128)S(1)}, f32[4,32,512]{2,1,0:T(8,128)S(1)}, f32[32,512]{1,0:T(8,128)S(1)}, s32[]{:T(128)}) %tuple.47), condition=%wide.region_2.3_spmd, body=%wide.region_1.2_spmd.sunk | while | flops 2343458 | bytes 3628701 | solution.py:163
  58.8 4.5 %collective-permute-start.1 = (f32[4,1,512]{2,1,0:T(1,128)S(1)}, f32[4,1,512]{2,1,0:T(1,128)S(1)}, u32[]{:S(2)}, u32[]{:S(2)}) collective-permute-start(f32[4,1,512]{2,1,0:T(1,128)S(1)} %get-tuple-element.93), channel_id=1, source_target_pairs={{0,8},{8,16},{16,24},{1,9},{9,17},{17,25},{2,10},{10,18},{18,26},{... | collective-permute-start | bytes 24584 | tf_op jit(solution)/shard_map/while/body/eval_jaxpr/ppermute | solution.py:33
  63.4 1.3 collective-permute-done.1
  66.2 3.0 collective-permute-start.3
  72.1 4.8 %collective-permute-start.1 = (f32[4,1,512]{2,1,0:T(1,128)S(1)}, f32[4,1,512]{2,1,0:T(1,128)S(1)}, u32[]{:S(2)}, u32[]{:S(2)}) collective-permute-start(f32[4,1,512]{2,1,0:T(1,128)S(1)} %get-tuple-element.93), channel_id=1, source_target_pairs={{0,8},{8,16},{16,24},{1,9},{9,17},{17,25},{2,10},{10,18},{18,26},{... | collective-permute-start | bytes 24584 | tf_op jit(solution)/shard_map/while/body/eval_jaxpr/ppermute | solution.py:33
  77.0 1.3 collective-permute-done.1
  79.7 3.0 collective-permute-start.3
  85.7 4.8 %collective-permute-start.1 = (f32[4,1,512]{2,1,0:T(1,128)S(1)}, f32[4,1,512]{2,1,0:T(1,128)S(1)}, u32[]{:S(2)}, u32[]{:S(2)}) collective-permute-start(f32[4,1,512]{2,1,0:T(1,128)S(1)} %get-tuple-element.93), channel_id=1, source_target_pairs={{0,8},{8,16},{16,24},{1,9},{9,17},{17,25},{2,10},{10,18},{18,26},{... | collective-permute-start | bytes 24584 | tf_op jit(solution)/shard_map/while/body/eval_jaxpr/ppermute | solution.py:33
  90.5 1.3 collective-permute-done.1
  93.3 4.8 %collective-permute-start.3 = (f32[4,34,1]{2,1,0:T(8,128)S(1)}, f32[4,34,1]{2,1,0:T(8,128)S(1)}, u32[]{:S(2)}, u32[]{:S(2)}) collective-permute-start(f32[4,34,1]{2,1,0:T(8,128)S(1)} %get-tuple-element.95), channel_id=1, source_target_pairs={{0,1},{1,2},{2,3},{3,4},{4,5},{5,6},{6,7},{8,9},{9,10},{10,11},{11... | collective-permute-start | bytes 1640 | tf_op jit(solution)/shard_map/while/body/eval_jaxpr/ppermute | solution.py:33
  101.0 4.5 %collective-permute-start.1 = (f32[4,1,512]{2,1,0:T(1,128)S(1)}, f32[4,1,512]{2,1,0:T(1,128)S(1)}, u32[]{:S(2)}, u32[]{:S(2)}) collective-permute-start(f32[4,1,512]{2,1,0:T(1,128)S(1)} %get-tuple-element.93), channel_id=1, source_target_pairs={{0,8},{8,16},{16,24},{1,9},{9,17},{17,25},{2,10},{10,18},{18,26},{... | collective-permute-start | bytes 24584 | tf_op jit(solution)/shard_map/while/body/eval_jaxpr/ppermute | solution.py:33
  105.6 1.3 collective-permute-done.1
  108.3 5.8 %collective-permute-start.3 = (f32[4,34,1]{2,1,0:T(8,128)S(1)}, f32[4,34,1]{2,1,0:T(8,128)S(1)}, u32[]{:S(2)}, u32[]{:S(2)}) collective-permute-start(f32[4,34,1]{2,1,0:T(8,128)S(1)} %get-tuple-element.95), channel_id=1, source_target_pairs={{0,1},{1,2},{2,3},{3,4},{4,5},{5,6},{6,7},{8,9},{9,10},{10,11},{11... | collective-permute-start | bytes 1640 | tf_op jit(solution)/shard_map/while/body/eval_jaxpr/ppermute | solution.py:33
  117.0 4.5 %collective-permute-start.1 = (f32[4,1,512]{2,1,0:T(1,128)S(1)}, f32[4,1,512]{2,1,0:T(1,128)S(1)}, u32[]{:S(2)}, u32[]{:S(2)}) collective-permute-start(f32[4,1,512]{2,1,0:T(1,128)S(1)} %get-tuple-element.93), channel_id=1, source_target_pairs={{0,8},{8,16},{16,24},{1,9},{9,17},{17,25},{2,10},{10,18},{18,26},{... | collective-permute-start | bytes 24584 | tf_op jit(solution)/shard_map/while/body/eval_jaxpr/ppermute | solution.py:33
  121.5 1.3 collective-permute-done.1
  124.3 5.8 %collective-permute-start.3 = (f32[4,34,1]{2,1,0:T(8,128)S(1)}, f32[4,34,1]{2,1,0:T(8,128)S(1)}, u32[]{:S(2)}, u32[]{:S(2)}) collective-permute-start(f32[4,34,1]{2,1,0:T(8,128)S(1)} %get-tuple-element.95), channel_id=1, source_target_pairs={{0,1},{1,2},{2,3},{3,4},{4,5},{5,6},{6,7},{8,9},{9,10},{10,11},{11... | collective-permute-start | bytes 1640 | tf_op jit(solution)/shard_map/while/body/eval_jaxpr/ppermute | solution.py:33
  133.0 4.5 %collective-permute-start.1 = (f32[4,1,512]{2,1,0:T(1,128)S(1)}, f32[4,1,512]{2,1,0:T(1,128)S(1)}, u32[]{:S(2)}, u32[]{:S(2)}) collective-permute-start(f32[4,1,512]{2,1,0:T(1,128)S(1)} %get-tuple-element.93), channel_id=1, source_target_pairs={{0,8},{8,16},{16,24},{1,9},{9,17},{17,25},{2,10},{10,18},{18,26},{... | collective-permute-start | bytes 24584 | tf_op jit(solution)/shard_map/while/body/eval_jaxpr/ppermute | solution.py:33
  137.6 1.3 collective-permute-done.1
  140.3 5.8 %collective-permute-start.3 = (f32[4,34,1]{2,1,0:T(8,128)S(1)}, f32[4,34,1]{2,1,0:T(8,128)S(1)}, u32[]{:S(2)}, u32[]{:S(2)}) collective-permute-start(f32[4,34,1]{2,1,0:T(8,128)S(1)} %get-tuple-element.95), channel_id=1, source_target_pairs={{0,1},{1,2},{2,3},{3,4},{4,5},{5,6},{6,7},{8,9},{9,10},{10,11},{11... | collective-permute-start | bytes 1640 | tf_op jit(solution)/shard_map/while/body/eval_jaxpr/ppermute | solution.py:33
  149.0 4.5 %collective-permute-start.1 = (f32[4,1,512]{2,1,0:T(1,128)S(1)}, f32[4,1,512]{2,1,0:T(1,128)S(1)}, u32[]{:S(2)}, u32[]{:S(2)}) collective-permute-start(f32[4,1,512]{2,1,0:T(1,128)S(1)} %get-tuple-element.93), channel_id=1, source_target_pairs={{0,8},{8,16},{16,24},{1,9},{9,17},{17,25},{2,10},{10,18},{18,26},{... | collective-permute-start | bytes 24584 | tf_op jit(solution)/shard_map/while/body/eval_jaxpr/ppermute | solution.py:33
  153.6 1.3 collective-permute-done.1
  156.3 5.8 %collective-permute-start.3 = (f32[4,34,1]{2,1,0:T(8,128)S(1)}, f32[4,34,1]{2,1,0:T(8,128)S(1)}, u32[]{:S(2)}, u32[]{:S(2)}) collective-permute-start(f32[4,34,1]{2,1,0:T(8,128)S(1)} %get-tuple-element.95), channel_id=1, source_target_pairs={{0,1},{1,2},{2,3},{3,4},{4,5},{5,6},{6,7},{8,9},{9,10},{10,11},{11... | collective-permute-start | bytes 1640 | tf_op jit(solution)/shard_map/while/body/eval_jaxpr/ppermute | solution.py:33
  165.0 4.5 %collective-permute-start.1 = (f32[4,1,512]{2,1,0:T(1,128)S(1)}, f32[4,1,512]{2,1,0:T(1,128)S(1)}, u32[]{:S(2)}, u32[]{:S(2)}) collective-permute-start(f32[4,1,512]{2,1,0:T(1,128)S(1)} %get-tuple-element.93), channel_id=1, source_target_pairs={{0,8},{8,16},{16,24},{1,9},{9,17},{17,25},{2,10},{10,18},{18,26},{... | collective-permute-start | bytes 24584 | tf_op jit(solution)/shard_map/while/body/eval_jaxpr/ppermute | solution.py:33
  169.6 1.3 collective-permute-done.1
  172.3 5.8 %collective-permute-start.3 = (f32[4,34,1]{2,1,0:T(8,128)S(1)}, f32[4,34,1]{2,1,0:T(8,128)S(1)}, u32[]{:S(2)}, u32[]{:S(2)}) collective-permute-start(f32[4,34,1]{2,1,0:T(8,128)S(1)} %get-tuple-element.95), channel_id=1, source_target_pairs={{0,1},{1,2},{2,3},{3,4},{4,5},{5,6},{6,7},{8,9},{9,10},{10,11},{11... | collective-permute-start | bytes 1640 | tf_op jit(solution)/shard_map/while/body/eval_jaxpr/ppermute | solution.py:33
  181.0 4.5 %collective-permute-start.1 = (f32[4,1,512]{2,1,0:T(1,128)S(1)}, f32[4,1,512]{2,1,0:T(1,128)S(1)}, u32[]{:S(2)}, u32[]{:S(2)}) collective-permute-start(f32[4,1,512]{2,1,0:T(1,128)S(1)} %get-tuple-element.93), channel_id=1, source_target_pairs={{0,8},{8,16},{16,24},{1,9},{9,17},{17,25},{2,10},{10,18},{18,26},{... | collective-permute-start | bytes 24584 | tf_op jit(solution)/shard_map/while/body/eval_jaxpr/ppermute | solution.py:33
  185.6 1.3 collective-permute-done.1
  188.3 5.8 %collective-permute-start.3 = (f32[4,34,1]{2,1,0:T(8,128)S(1)}, f32[4,34,1]{2,1,0:T(8,128)S(1)}, u32[]{:S(2)}, u32[]{:S(2)}) collective-permute-start(f32[4,34,1]{2,1,0:T(8,128)S(1)} %get-tuple-element.95), channel_id=1, source_target_pairs={{0,1},{1,2},{2,3},{3,4},{4,5},{5,6},{6,7},{8,9},{9,10},{10,11},{11... | collective-permute-start | bytes 1640 | tf_op jit(solution)/shard_map/while/body/eval_jaxpr/ppermute | solution.py:33
  197.0 4.5 %collective-permute-start.1 = (f32[4,1,512]{2,1,0:T(1,128)S(1)}, f32[4,1,512]{2,1,0:T(1,128)S(1)}, u32[]{:S(2)}, u32[]{:S(2)}) collective-permute-start(f32[4,1,512]{2,1,0:T(1,128)S(1)} %get-tuple-element.93), channel_id=1, source_target_pairs={{0,8},{8,16},{16,24},{1,9},{9,17},{17,25},{2,10},{10,18},{18,26},{... | collective-permute-start | bytes 24584 | tf_op jit(solution)/shard_map/while/body/eval_jaxpr/ppermute | solution.py:33
  201.6 1.3 collective-permute-done.1
  204.3 6.2 %collective-permute-start.3 = (f32[4,34,1]{2,1,0:T(8,128)S(1)}, f32[4,34,1]{2,1,0:T(8,128)S(1)}, u32[]{:S(2)}, u32[]{:S(2)}) collective-permute-start(f32[4,34,1]{2,1,0:T(8,128)S(1)} %get-tuple-element.95), channel_id=1, source_target_pairs={{0,1},{1,2},{2,3},{3,4},{4,5},{5,6},{6,7},{8,9},{9,10},{10,11},{11... | collective-permute-start | bytes 1640 | tf_op jit(solution)/shard_map/while/body/eval_jaxpr/ppermute | solution.py:33
  213.5 4.5 %collective-permute-start.1 = (f32[4,1,512]{2,1,0:T(1,128)S(1)}, f32[4,1,512]{2,1,0:T(1,128)S(1)}, u32[]{:S(2)}, u32[]{:S(2)}) collective-permute-start(f32[4,1,512]{2,1,0:T(1,128)S(1)} %get-tuple-element.93), channel_id=1, source_target_pairs={{0,8},{8,16},{16,24},{1,9},{9,17},{17,25},{2,10},{10,18},{18,26},{... | collective-permute-start | bytes 24584 | tf_op jit(solution)/shard_map/while/body/eval_jaxpr/ppermute | solution.py:33
  218.1 1.3 collective-permute-done.1
  220.8 6.6 %collective-permute-start.3 = (f32[4,34,1]{2,1,0:T(8,128)S(1)}, f32[4,34,1]{2,1,0:T(8,128)S(1)}, u32[]{:S(2)}, u32[]{:S(2)}) collective-permute-start(f32[4,34,1]{2,1,0:T(8,128)S(1)} %get-tuple-element.95), channel_id=1, source_target_pairs={{0,1},{1,2},{2,3},{3,4},{4,5},{5,6},{6,7},{8,9},{9,10},{10,11},{11... | collective-permute-start | bytes 1640 | tf_op jit(solution)/shard_map/while/body/eval_jaxpr/ppermute | solution.py:33
  230.4 4.5 %collective-permute-start.1 = (f32[4,1,512]{2,1,0:T(1,128)S(1)}, f32[4,1,512]{2,1,0:T(1,128)S(1)}, u32[]{:S(2)}, u32[]{:S(2)}) collective-permute-start(f32[4,1,512]{2,1,0:T(1,128)S(1)} %get-tuple-element.93), channel_id=1, source_target_pairs={{0,8},{8,16},{16,24},{1,9},{9,17},{17,25},{2,10},{10,18},{18,26},{... | collective-permute-start | bytes 24584 | tf_op jit(solution)/shard_map/while/body/eval_jaxpr/ppermute | solution.py:33
  237.7 6.6 %collective-permute-start.3 = (f32[4,34,1]{2,1,0:T(8,128)S(1)}, f32[4,34,1]{2,1,0:T(8,128)S(1)}, u32[]{:S(2)}, u32[]{:S(2)}) collective-permute-start(f32[4,34,1]{2,1,0:T(8,128)S(1)} %get-tuple-element.95), channel_id=1, source_target_pairs={{0,1},{1,2},{2,3},{3,4},{4,5},{5,6},{6,7},{8,9},{9,10},{10,11},{11... | collective-permute-start | bytes 1640 | tf_op jit(solution)/shard_map/while/body/eval_jaxpr/ppermute | solution.py:33
  247.3 4.5 %collective-permute-start.1 = (f32[4,1,512]{2,1,0:T(1,128)S(1)}, f32[4,1,512]{2,1,0:T(1,128)S(1)}, u32[]{:S(2)}, u32[]{:S(2)}) collective-permute-start(f32[4,1,512]{2,1,0:T(1,128)S(1)} %get-tuple-element.93), channel_id=1, source_target_pairs={{0,8},{8,16},{16,24},{1,9},{9,17},{17,25},{2,10},{10,18},{18,26},{... | collective-permute-start | bytes 24584 | tf_op jit(solution)/shard_map/while/body/eval_jaxpr/ppermute | solution.py:33
  254.6 6.6 %collective-permute-start.3 = (f32[4,34,1]{2,1,0:T(8,128)S(1)}, f32[4,34,1]{2,1,0:T(8,128)S(1)}, u32[]{:S(2)}, u32[]{:S(2)}) collective-permute-start(f32[4,34,1]{2,1,0:T(8,128)S(1)} %get-tuple-element.95), channel_id=1, source_target_pairs={{0,1},{1,2},{2,3},{3,4},{4,5},{5,6},{6,7},{8,9},{9,10},{10,11},{11... | collective-permute-start | bytes 1640 | tf_op jit(solution)/shard_map/while/body/eval_jaxpr/ppermute | solution.py:33
  264.2 4.5 %collective-permute-start.1 = (f32[4,1,512]{2,1,0:T(1,128)S(1)}, f32[4,1,512]{2,1,0:T(1,128)S(1)}, u32[]{:S(2)}, u32[]{:S(2)}) collective-permute-start(f32[4,1,512]{2,1,0:T(1,128)S(1)} %get-tuple-element.93), channel_id=1, source_target_pairs={{0,8},{8,16},{16,24},{1,9},{9,17},{17,25},{2,10},{10,18},{18,26},{... | collective-permute-start | bytes 24584 | tf_op jit(solution)/shard_map/while/body/eval_jaxpr/ppermute | solution.py:33
  271.5 6.6 %collective-permute-start.3 = (f32[4,34,1]{2,1,0:T(8,128)S(1)}, f32[4,34,1]{2,1,0:T(8,128)S(1)}, u32[]{:S(2)}, u32[]{:S(2)}) collective-permute-start(f32[4,34,1]{2,1,0:T(8,128)S(1)} %get-tuple-element.95), channel_id=1, source_target_pairs={{0,1},{1,2},{2,3},{3,4},{4,5},{5,6},{6,7},{8,9},{9,10},{10,11},{11... | collective-permute-start | bytes 1640 | tf_op jit(solution)/shard_map/while/body/eval_jaxpr/ppermute | solution.py:33
  281.1 4.5 %collective-permute-start.1 = (f32[4,1,512]{2,1,0:T(1,128)S(1)}, f32[4,1,512]{2,1,0:T(1,128)S(1)}, u32[]{:S(2)}, u32[]{:S(2)}) collective-permute-start(f32[4,1,512]{2,1,0:T(1,128)S(1)} %get-tuple-element.93), channel_id=1, source_target_pairs={{0,8},{8,16},{16,24},{1,9},{9,17},{17,25},{2,10},{10,18},{18,26},{... | collective-permute-start | bytes 24584 | tf_op jit(solution)/shard_map/while/body/eval_jaxpr/ppermute | solution.py:33
  288.4 6.6 %collective-permute-start.3 = (f32[4,34,1]{2,1,0:T(8,128)S(1)}, f32[4,34,1]{2,1,0:T(8,128)S(1)}, u32[]{:S(2)}, u32[]{:S(2)}) collective-permute-start(f32[4,34,1]{2,1,0:T(8,128)S(1)} %get-tuple-element.95), channel_id=1, source_target_pairs={{0,1},{1,2},{2,3},{3,4},{4,5},{5,6},{6,7},{8,9},{9,10},{10,11},{11... | collective-permute-start | bytes 1640 | tf_op jit(solution)/shard_map/while/body/eval_jaxpr/ppermute | solution.py:33
  298.0 4.5 %collective-permute-start.1 = (f32[4,1,512]{2,1,0:T(1,128)S(1)}, f32[4,1,512]{2,1,0:T(1,128)S(1)}, u32[]{:S(2)}, u32[]{:S(2)}) collective-permute-start(f32[4,1,512]{2,1,0:T(1,128)S(1)} %get-tuple-element.93), channel_id=1, source_target_pairs={{0,8},{8,16},{16,24},{1,9},{9,17},{17,25},{2,10},{10,18},{18,26},{... | collective-permute-start | bytes 24584 | tf_op jit(solution)/shard_map/while/body/eval_jaxpr/ppermute | solution.py:33
  305.3 6.6 %collective-permute-start.3 = (f32[4,34,1]{2,1,0:T(8,128)S(1)}, f32[4,34,1]{2,1,0:T(8,128)S(1)}, u32[]{:S(2)}, u32[]{:S(2)}) collective-permute-start(f32[4,34,1]{2,1,0:T(8,128)S(1)} %get-tuple-element.95), channel_id=1, source_target_pairs={{0,1},{1,2},{2,3},{3,4},{4,5},{5,6},{6,7},{8,9},{9,10},{10,11},{11... | collective-permute-start | bytes 1640 | tf_op jit(solution)/shard_map/while/body/eval_jaxpr/ppermute | solution.py:33
  314.9 4.5 %collective-permute-start.1 = (f32[4,1,512]{2,1,0:T(1,128)S(1)}, f32[4,1,512]{2,1,0:T(1,128)S(1)}, u32[]{:S(2)}, u32[]{:S(2)}) collective-permute-start(f32[4,1,512]{2,1,0:T(1,128)S(1)} %get-tuple-element.93), channel_id=1, source_target_pairs={{0,8},{8,16},{16,24},{1,9},{9,17},{17,25},{2,10},{10,18},{18,26},{... | collective-permute-start | bytes 24584 | tf_op jit(solution)/shard_map/while/body/eval_jaxpr/ppermute | solution.py:33
  322.2 6.6 %collective-permute-start.3 = (f32[4,34,1]{2,1,0:T(8,128)S(1)}, f32[4,34,1]{2,1,0:T(8,128)S(1)}, u32[]{:S(2)}, u32[]{:S(2)}) collective-permute-start(f32[4,34,1]{2,1,0:T(8,128)S(1)} %get-tuple-element.95), channel_id=1, source_target_pairs={{0,1},{1,2},{2,3},{3,4},{4,5},{5,6},{6,7},{8,9},{9,10},{10,11},{11... | collective-permute-start | bytes 1640 | tf_op jit(solution)/shard_map/while/body/eval_jaxpr/ppermute | solution.py:33
  331.8 4.5 %collective-permute-start.1 = (f32[4,1,512]{2,1,0:T(1,128)S(1)}, f32[4,1,512]{2,1,0:T(1,128)S(1)}, u32[]{:S(2)}, u32[]{:S(2)}) collective-permute-start(f32[4,1,512]{2,1,0:T(1,128)S(1)} %get-tuple-element.93), channel_id=1, source_target_pairs={{0,8},{8,16},{16,24},{1,9},{9,17},{17,25},{2,10},{10,18},{18,26},{... | collective-permute-start | bytes 24584 | tf_op jit(solution)/shard_map/while/body/eval_jaxpr/ppermute | solution.py:33
  339.1 6.6 %collective-permute-start.3 = (f32[4,34,1]{2,1,0:T(8,128)S(1)}, f32[4,34,1]{2,1,0:T(8,128)S(1)}, u32[]{:S(2)}, u32[]{:S(2)}) collective-permute-start(f32[4,34,1]{2,1,0:T(8,128)S(1)} %get-tuple-element.95), channel_id=1, source_target_pairs={{0,1},{1,2},{2,3},{3,4},{4,5},{5,6},{6,7},{8,9},{9,10},{10,11},{11... | collective-permute-start | bytes 1640 | tf_op jit(solution)/shard_map/while/body/eval_jaxpr/ppermute | solution.py:33
  348.7 4.5 %collective-permute-start.1 = (f32[4,1,512]{2,1,0:T(1,128)S(1)}, f32[4,1,512]{2,1,0:T(1,128)S(1)}, u32[]{:S(2)}, u32[]{:S(2)}) collective-permute-start(f32[4,1,512]{2,1,0:T(1,128)S(1)} %get-tuple-element.93), channel_id=1, source_target_pairs={{0,8},{8,16},{16,24},{1,9},{9,17},{17,25},{2,10},{10,18},{18,26},{... | collective-permute-start | bytes 24584 | tf_op jit(solution)/shard_map/while/body/eval_jaxpr/ppermute | solution.py:33
  356.0 6.6 %collective-permute-start.3 = (f32[4,34,1]{2,1,0:T(8,128)S(1)}, f32[4,34,1]{2,1,0:T(8,128)S(1)}, u32[]{:S(2)}, u32[]{:S(2)}) collective-permute-start(f32[4,34,1]{2,1,0:T(8,128)S(1)} %get-tuple-element.95), channel_id=1, source_target_pairs={{0,1},{1,2},{2,3},{3,4},{4,5},{5,6},{6,7},{8,9},{9,10},{10,11},{11... | collective-permute-start | bytes 1640 | tf_op jit(solution)/shard_map/while/body/eval_jaxpr/ppermute | solution.py:33
  365.6 4.5 %collective-permute-start.1 = (f32[4,1,512]{2,1,0:T(1,128)S(1)}, f32[4,1,512]{2,1,0:T(1,128)S(1)}, u32[]{:S(2)}, u32[]{:S(2)}) collective-permute-start(f32[4,1,512]{2,1,0:T(1,128)S(1)} %get-tuple-element.93), channel_id=1, source_target_pairs={{0,8},{8,16},{16,24},{1,9},{9,17},{17,25},{2,10},{10,18},{18,26},{... | collective-permute-start | bytes 24584 | tf_op jit(solution)/shard_map/while/body/eval_jaxpr/ppermute | solution.py:33
  372.9 6.6 %collective-permute-start.3 = (f32[4,34,1]{2,1,0:T(8,128)S(1)}, f32[4,34,1]{2,1,0:T(8,128)S(1)}, u32[]{:S(2)}, u32[]{:S(2)}) collective-permute-start(f32[4,34,1]{2,1,0:T(8,128)S(1)} %get-tuple-element.95), channel_id=1, source_target_pairs={{0,1},{1,2},{2,3},{3,4},{4,5},{5,6},{6,7},{8,9},{9,10},{10,11},{11... | collective-permute-start | bytes 1640 | tf_op jit(solution)/shard_map/while/body/eval_jaxpr/ppermute | solution.py:33
  382.1 22.1 %scatter_fusion.1 = s32[8,16]{1,0:T(8,128)S(1)} fusion(s32[8,16]{1,0:T(8,128)S(1)} %broadcast.610, s32[512]{0:T(512)S(1)} %reshape.641, s32[512]{0:T(512)S(1)} %reshape.643), kind=kCustom, calls=%fused_computation.5 | custom fusion | bytes 10240 | tf_op jit(solution)/shard_map/scatter | solution.py:156
  404.3 1.4 gather_fusion
  405.8 15.8 %all-to-all-start = ((f32[8,16,512]{2,1,0:T(8,128)}), f32[8,16,512]{2,1,0:T(8,128)S(1)}, u32[]{:S(2)}, u32[]{:S(2)}) async-start(f32[8,16,512]{2,1,0:T(8,128)} %bitcast.26), calls=%async_computation | async-start | bytes 524288 | tf_op jit(solution)/shard_map/all_to_all | solution.py:165
  421.6 2.5 reduce_sum.22
  425.5 3.0 all-to-all-done
  429.4 6.2 %fusion.35 = f32[64,8,256]{2,0,1:T(8,128)S(1)} fusion(f32[8,256,512]{2,1,0:T(8,128)} %param.12, f32[64,512]{1,0:T(8,128)S(1)} %gather_fusion.1), kind=kOutput, calls=%fused_computation.71 | convolution fusion | flops 805306368 | bytes 4849664 | tf_op jit(solution)/shard_map/ko,wao->kwa/dot_general | solution.py:167
  (282 shorter events, 105.3 us)
Async XLA Ops:
  57.5 5.9 %collective-permute-start = (f32[4,1,512]{2,1,0:T(1,128)S(1)}, f32[4,1,512]{2,1,0:T(1,128)S(1)}, u32[]{:S(2)}, u32[]{:S(2)}) collective-permute-start(f32[4,1,512]{2,1,0:T(1,128)S(1)} %get-tuple-element.92), channel_id=1, source_target_pairs={{8,0},{16,8},{24,16},{9,1},{17,9},{25,17},{10,2},{18,10},{26,18},{... | collective-permute-start | bytes 24584 | tf_op jit(solution)/shard_map/while/body/eval_jaxpr/ppermute | solution.py:34
  58.8 5.9 %collective-permute-start.1 = (f32[4,1,512]{2,1,0:T(1,128)S(1)}, f32[4,1,512]{2,1,0:T(1,128)S(1)}, u32[]{:S(2)}, u32[]{:S(2)}) collective-permute-start(f32[4,1,512]{2,1,0:T(1,128)S(1)} %get-tuple-element.93), channel_id=1, source_target_pairs={{0,8},{8,16},{16,24},{1,9},{9,17},{17,25},{2,10},{10,18},{18,26},{... | collective-permute-start | bytes 24584 | tf_op jit(solution)/shard_map/while/body/eval_jaxpr/ppermute | solution.py:33
  70.8 6.1 %collective-permute-start = (f32[4,1,512]{2,1,0:T(1,128)S(1)}, f32[4,1,512]{2,1,0:T(1,128)S(1)}, u32[]{:S(2)}, u32[]{:S(2)}) collective-permute-start(f32[4,1,512]{2,1,0:T(1,128)S(1)} %get-tuple-element.92), channel_id=1, source_target_pairs={{8,0},{16,8},{24,16},{9,1},{17,9},{25,17},{10,2},{18,10},{26,18},{... | collective-permute-start | bytes 24584 | tf_op jit(solution)/shard_map/while/body/eval_jaxpr/ppermute | solution.py:34
  72.1 6.2 %collective-permute-start.1 = (f32[4,1,512]{2,1,0:T(1,128)S(1)}, f32[4,1,512]{2,1,0:T(1,128)S(1)}, u32[]{:S(2)}, u32[]{:S(2)}) collective-permute-start(f32[4,1,512]{2,1,0:T(1,128)S(1)} %get-tuple-element.93), channel_id=1, source_target_pairs={{0,8},{8,16},{16,24},{1,9},{9,17},{17,25},{2,10},{10,18},{18,26},{... | collective-permute-start | bytes 24584 | tf_op jit(solution)/shard_map/while/body/eval_jaxpr/ppermute | solution.py:33
  84.4 6.1 %collective-permute-start = (f32[4,1,512]{2,1,0:T(1,128)S(1)}, f32[4,1,512]{2,1,0:T(1,128)S(1)}, u32[]{:S(2)}, u32[]{:S(2)}) collective-permute-start(f32[4,1,512]{2,1,0:T(1,128)S(1)} %get-tuple-element.92), channel_id=1, source_target_pairs={{8,0},{16,8},{24,16},{9,1},{17,9},{25,17},{10,2},{18,10},{26,18},{... | collective-permute-start | bytes 24584 | tf_op jit(solution)/shard_map/while/body/eval_jaxpr/ppermute | solution.py:34
  85.7 6.2 %collective-permute-start.1 = (f32[4,1,512]{2,1,0:T(1,128)S(1)}, f32[4,1,512]{2,1,0:T(1,128)S(1)}, u32[]{:S(2)}, u32[]{:S(2)}) collective-permute-start(f32[4,1,512]{2,1,0:T(1,128)S(1)} %get-tuple-element.93), channel_id=1, source_target_pairs={{0,8},{8,16},{16,24},{1,9},{9,17},{17,25},{2,10},{10,18},{18,26},{... | collective-permute-start | bytes 24584 | tf_op jit(solution)/shard_map/while/body/eval_jaxpr/ppermute | solution.py:33
  92.0 6.1 %collective-permute-start.2 = (f32[4,34,1]{2,1,0:T(8,128)S(1)}, f32[4,34,1]{2,1,0:T(8,128)S(1)}, u32[]{:S(2)}, u32[]{:S(2)}) collective-permute-start(f32[4,34,1]{2,1,0:T(8,128)S(1)} %get-tuple-element.94), channel_id=1, source_target_pairs={{1,0},{2,1},{3,2},{4,3},{5,4},{6,5},{7,6},{9,8},{10,9},{11,10},{12... | collective-permute-start | bytes 1640 | tf_op jit(solution)/shard_map/while/body/eval_jaxpr/ppermute | solution.py:34
  99.7 5.9 %collective-permute-start = (f32[4,1,512]{2,1,0:T(1,128)S(1)}, f32[4,1,512]{2,1,0:T(1,128)S(1)}, u32[]{:S(2)}, u32[]{:S(2)}) collective-permute-start(f32[4,1,512]{2,1,0:T(1,128)S(1)} %get-tuple-element.92), channel_id=1, source_target_pairs={{8,0},{16,8},{24,16},{9,1},{17,9},{25,17},{10,2},{18,10},{26,18},{... | collective-permute-start | bytes 24584 | tf_op jit(solution)/shard_map/while/body/eval_jaxpr/ppermute | solution.py:34
  101.0 5.9 %collective-permute-start.1 = (f32[4,1,512]{2,1,0:T(1,128)S(1)}, f32[4,1,512]{2,1,0:T(1,128)S(1)}, u32[]{:S(2)}, u32[]{:S(2)}) collective-permute-start(f32[4,1,512]{2,1,0:T(1,128)S(1)} %get-tuple-element.93), channel_id=1, source_target_pairs={{0,8},{8,16},{16,24},{1,9},{9,17},{17,25},{2,10},{10,18},{18,26},{... | collective-permute-start | bytes 24584 | tf_op jit(solution)/shard_map/while/body/eval_jaxpr/ppermute | solution.py:33
  107.0 7.1 %collective-permute-start.2 = (f32[4,34,1]{2,1,0:T(8,128)S(1)}, f32[4,34,1]{2,1,0:T(8,128)S(1)}, u32[]{:S(2)}, u32[]{:S(2)}) collective-permute-start(f32[4,34,1]{2,1,0:T(8,128)S(1)} %get-tuple-element.94), channel_id=1, source_target_pairs={{1,0},{2,1},{3,2},{4,3},{5,4},{6,5},{7,6},{9,8},{10,9},{11,10},{12... | collective-permute-start | bytes 1640 | tf_op jit(solution)/shard_map/while/body/eval_jaxpr/ppermute | solution.py:34
  108.3 6.7 %collective-permute-start.3 = (f32[4,34,1]{2,1,0:T(8,128)S(1)}, f32[4,34,1]{2,1,0:T(8,128)S(1)}, u32[]{:S(2)}, u32[]{:S(2)}) collective-permute-start(f32[4,34,1]{2,1,0:T(8,128)S(1)} %get-tuple-element.95), channel_id=1, source_target_pairs={{0,1},{1,2},{2,3},{3,4},{4,5},{5,6},{6,7},{8,9},{9,10},{10,11},{11... | collective-permute-start | bytes 1640 | tf_op jit(solution)/shard_map/while/body/eval_jaxpr/ppermute | solution.py:33
  115.7 5.9 %collective-permute-start = (f32[4,1,512]{2,1,0:T(1,128)S(1)}, f32[4,1,512]{2,1,0:T(1,128)S(1)}, u32[]{:S(2)}, u32[]{:S(2)}) collective-permute-start(f32[4,1,512]{2,1,0:T(1,128)S(1)} %get-tuple-element.92), channel_id=1, source_target_pairs={{8,0},{16,8},{24,16},{9,1},{17,9},{25,17},{10,2},{18,10},{26,18},{... | collective-permute-start | bytes 24584 | tf_op jit(solution)/shard_map/while/body/eval_jaxpr/ppermute | solution.py:34
  117.0 5.9 %collective-permute-start.1 = (f32[4,1,512]{2,1,0:T(1,128)S(1)}, f32[4,1,512]{2,1,0:T(1,128)S(1)}, u32[]{:S(2)}, u32[]{:S(2)}) collective-permute-start(f32[4,1,512]{2,1,0:T(1,128)S(1)} %get-tuple-element.93), channel_id=1, source_target_pairs={{0,8},{8,16},{16,24},{1,9},{9,17},{17,25},{2,10},{10,18},{18,26},{... | collective-permute-start | bytes 24584 | tf_op jit(solution)/shard_map/while/body/eval_jaxpr/ppermute | solution.py:33
  123.0 7.1 %collective-permute-start.2 = (f32[4,34,1]{2,1,0:T(8,128)S(1)}, f32[4,34,1]{2,1,0:T(8,128)S(1)}, u32[]{:S(2)}, u32[]{:S(2)}) collective-permute-start(f32[4,34,1]{2,1,0:T(8,128)S(1)} %get-tuple-element.94), channel_id=1, source_target_pairs={{1,0},{2,1},{3,2},{4,3},{5,4},{6,5},{7,6},{9,8},{10,9},{11,10},{12... | collective-permute-start | bytes 1640 | tf_op jit(solution)/shard_map/while/body/eval_jaxpr/ppermute | solution.py:34
  124.3 6.7 %collective-permute-start.3 = (f32[4,34,1]{2,1,0:T(8,128)S(1)}, f32[4,34,1]{2,1,0:T(8,128)S(1)}, u32[]{:S(2)}, u32[]{:S(2)}) collective-permute-start(f32[4,34,1]{2,1,0:T(8,128)S(1)} %get-tuple-element.95), channel_id=1, source_target_pairs={{0,1},{1,2},{2,3},{3,4},{4,5},{5,6},{6,7},{8,9},{9,10},{10,11},{11... | collective-permute-start | bytes 1640 | tf_op jit(solution)/shard_map/while/body/eval_jaxpr/ppermute | solution.py:33
  133.0 5.9 %collective-permute-start.1 = (f32[4,1,512]{2,1,0:T(1,128)S(1)}, f32[4,1,512]{2,1,0:T(1,128)S(1)}, u32[]{:S(2)}, u32[]{:S(2)}) collective-permute-start(f32[4,1,512]{2,1,0:T(1,128)S(1)} %get-tuple-element.93), channel_id=1, source_target_pairs={{0,8},{8,16},{16,24},{1,9},{9,17},{17,25},{2,10},{10,18},{18,26},{... | collective-permute-start | bytes 24584 | tf_op jit(solution)/shard_map/while/body/eval_jaxpr/ppermute | solution.py:33
  139.0 7.1 %collective-permute-start.2 = (f32[4,34,1]{2,1,0:T(8,128)S(1)}, f32[4,34,1]{2,1,0:T(8,128)S(1)}, u32[]{:S(2)}, u32[]{:S(2)}) collective-permute-start(f32[4,34,1]{2,1,0:T(8,128)S(1)} %get-tuple-element.94), channel_id=1, source_target_pairs={{1,0},{2,1},{3,2},{4,3},{5,4},{6,5},{7,6},{9,8},{10,9},{11,10},{12... | collective-permute-start | bytes 1640 | tf_op jit(solution)/shard_map/while/body/eval_jaxpr/ppermute | solution.py:34
  140.3 6.7 %collective-permute-start.3 = (f32[4,34,1]{2,1,0:T(8,128)S(1)}, f32[4,34,1]{2,1,0:T(8,128)S(1)}, u32[]{:S(2)}, u32[]{:S(2)}) collective-permute-start(f32[4,34,1]{2,1,0:T(8,128)S(1)} %get-tuple-element.95), channel_id=1, source_target_pairs={{0,1},{1,2},{2,3},{3,4},{4,5},{5,6},{6,7},{8,9},{9,10},{10,11},{11... | collective-permute-start | bytes 1640 | tf_op jit(solution)/shard_map/while/body/eval_jaxpr/ppermute | solution.py:33
  149.0 5.9 %collective-permute-start.1 = (f32[4,1,512]{2,1,0:T(1,128)S(1)}, f32[4,1,512]{2,1,0:T(1,128)S(1)}, u32[]{:S(2)}, u32[]{:S(2)}) collective-permute-start(f32[4,1,512]{2,1,0:T(1,128)S(1)} %get-tuple-element.93), channel_id=1, source_target_pairs={{0,8},{8,16},{16,24},{1,9},{9,17},{17,25},{2,10},{10,18},{18,26},{... | collective-permute-start | bytes 24584 | tf_op jit(solution)/shard_map/while/body/eval_jaxpr/ppermute | solution.py:33
  155.0 7.1 %collective-permute-start.2 = (f32[4,34,1]{2,1,0:T(8,128)S(1)}, f32[4,34,1]{2,1,0:T(8,128)S(1)}, u32[]{:S(2)}, u32[]{:S(2)}) collective-permute-start(f32[4,34,1]{2,1,0:T(8,128)S(1)} %get-tuple-element.94), channel_id=1, source_target_pairs={{1,0},{2,1},{3,2},{4,3},{5,4},{6,5},{7,6},{9,8},{10,9},{11,10},{12... | collective-permute-start | bytes 1640 | tf_op jit(solution)/shard_map/while/body/eval_jaxpr/ppermute | solution.py:34
  156.3 6.7 %collective-permute-start.3 = (f32[4,34,1]{2,1,0:T(8,128)S(1)}, f32[4,34,1]{2,1,0:T(8,128)S(1)}, u32[]{:S(2)}, u32[]{:S(2)}) collective-permute-start(f32[4,34,1]{2,1,0:T(8,128)S(1)} %get-tuple-element.95), channel_id=1, source_target_pairs={{0,1},{1,2},{2,3},{3,4},{4,5},{5,6},{6,7},{8,9},{9,10},{10,11},{11... | collective-permute-start | bytes 1640 | tf_op jit(solution)/shard_map/while/body/eval_jaxpr/ppermute | solution.py:33
  165.0 5.9 %collective-permute-start.1 = (f32[4,1,512]{2,1,0:T(1,128)S(1)}, f32[4,1,512]{2,1,0:T(1,128)S(1)}, u32[]{:S(2)}, u32[]{:S(2)}) collective-permute-start(f32[4,1,512]{2,1,0:T(1,128)S(1)} %get-tuple-element.93), channel_id=1, source_target_pairs={{0,8},{8,16},{16,24},{1,9},{9,17},{17,25},{2,10},{10,18},{18,26},{... | collective-permute-start | bytes 24584 | tf_op jit(solution)/shard_map/while/body/eval_jaxpr/ppermute | solution.py:33
  171.0 7.1 %collective-permute-start.2 = (f32[4,34,1]{2,1,0:T(8,128)S(1)}, f32[4,34,1]{2,1,0:T(8,128)S(1)}, u32[]{:S(2)}, u32[]{:S(2)}) collective-permute-start(f32[4,34,1]{2,1,0:T(8,128)S(1)} %get-tuple-element.94), channel_id=1, source_target_pairs={{1,0},{2,1},{3,2},{4,3},{5,4},{6,5},{7,6},{9,8},{10,9},{11,10},{12... | collective-permute-start | bytes 1640 | tf_op jit(solution)/shard_map/while/body/eval_jaxpr/ppermute | solution.py:34
  172.3 6.7 %collective-permute-start.3 = (f32[4,34,1]{2,1,0:T(8,128)S(1)}, f32[4,34,1]{2,1,0:T(8,128)S(1)}, u32[]{:S(2)}, u32[]{:S(2)}) collective-permute-start(f32[4,34,1]{2,1,0:T(8,128)S(1)} %get-tuple-element.95), channel_id=1, source_target_pairs={{0,1},{1,2},{2,3},{3,4},{4,5},{5,6},{6,7},{8,9},{9,10},{10,11},{11... | collective-permute-start | bytes 1640 | tf_op jit(solution)/shard_map/while/body/eval_jaxpr/ppermute | solution.py:33
  181.0 5.9 %collective-permute-start.1 = (f32[4,1,512]{2,1,0:T(1,128)S(1)}, f32[4,1,512]{2,1,0:T(1,128)S(1)}, u32[]{:S(2)}, u32[]{:S(2)}) collective-permute-start(f32[4,1,512]{2,1,0:T(1,128)S(1)} %get-tuple-element.93), channel_id=1, source_target_pairs={{0,8},{8,16},{16,24},{1,9},{9,17},{17,25},{2,10},{10,18},{18,26},{... | collective-permute-start | bytes 24584 | tf_op jit(solution)/shard_map/while/body/eval_jaxpr/ppermute | solution.py:33
  187.0 7.1 %collective-permute-start.2 = (f32[4,34,1]{2,1,0:T(8,128)S(1)}, f32[4,34,1]{2,1,0:T(8,128)S(1)}, u32[]{:S(2)}, u32[]{:S(2)}) collective-permute-start(f32[4,34,1]{2,1,0:T(8,128)S(1)} %get-tuple-element.94), channel_id=1, source_target_pairs={{1,0},{2,1},{3,2},{4,3},{5,4},{6,5},{7,6},{9,8},{10,9},{11,10},{12... | collective-permute-start | bytes 1640 | tf_op jit(solution)/shard_map/while/body/eval_jaxpr/ppermute | solution.py:34
  188.3 6.7 %collective-permute-start.3 = (f32[4,34,1]{2,1,0:T(8,128)S(1)}, f32[4,34,1]{2,1,0:T(8,128)S(1)}, u32[]{:S(2)}, u32[]{:S(2)}) collective-permute-start(f32[4,34,1]{2,1,0:T(8,128)S(1)} %get-tuple-element.95), channel_id=1, source_target_pairs={{0,1},{1,2},{2,3},{3,4},{4,5},{5,6},{6,7},{8,9},{9,10},{10,11},{11... | collective-permute-start | bytes 1640 | tf_op jit(solution)/shard_map/while/body/eval_jaxpr/ppermute | solution.py:33
  195.7 5.9 %collective-permute-start = (f32[4,1,512]{2,1,0:T(1,128)S(1)}, f32[4,1,512]{2,1,0:T(1,128)S(1)}, u32[]{:S(2)}, u32[]{:S(2)}) collective-permute-start(f32[4,1,512]{2,1,0:T(1,128)S(1)} %get-tuple-element.92), channel_id=1, source_target_pairs={{8,0},{16,8},{24,16},{9,1},{17,9},{25,17},{10,2},{18,10},{26,18},{... | collective-permute-start | bytes 24584 | tf_op jit(solution)/shard_map/while/body/eval_jaxpr/ppermute | solution.py:34
  197.0 5.9 %collective-permute-start.1 = (f32[4,1,512]{2,1,0:T(1,128)S(1)}, f32[4,1,512]{2,1,0:T(1,128)S(1)}, u32[]{:S(2)}, u32[]{:S(2)}) collective-permute-start(f32[4,1,512]{2,1,0:T(1,128)S(1)} %get-tuple-element.93), channel_id=1, source_target_pairs={{0,8},{8,16},{16,24},{1,9},{9,17},{17,25},{2,10},{10,18},{18,26},{... | collective-permute-start | bytes 24584 | tf_op jit(solution)/shard_map/while/body/eval_jaxpr/ppermute | solution.py:33
  203.0 7.5 %collective-permute-start.2 = (f32[4,34,1]{2,1,0:T(8,128)S(1)}, f32[4,34,1]{2,1,0:T(8,128)S(1)}, u32[]{:S(2)}, u32[]{:S(2)}) collective-permute-start(f32[4,34,1]{2,1,0:T(8,128)S(1)} %get-tuple-element.94), channel_id=1, source_target_pairs={{1,0},{2,1},{3,2},{4,3},{5,4},{6,5},{7,6},{9,8},{10,9},{11,10},{12... | collective-permute-start | bytes 1640 | tf_op jit(solution)/shard_map/while/body/eval_jaxpr/ppermute | solution.py:34
  204.3 7.1 %collective-permute-start.3 = (f32[4,34,1]{2,1,0:T(8,128)S(1)}, f32[4,34,1]{2,1,0:T(8,128)S(1)}, u32[]{:S(2)}, u32[]{:S(2)}) collective-permute-start(f32[4,34,1]{2,1,0:T(8,128)S(1)} %get-tuple-element.95), channel_id=1, source_target_pairs={{0,1},{1,2},{2,3},{3,4},{4,5},{5,6},{6,7},{8,9},{9,10},{10,11},{11... | collective-permute-start | bytes 1640 | tf_op jit(solution)/shard_map/while/body/eval_jaxpr/ppermute | solution.py:33
  212.2 5.9 %collective-permute-start = (f32[4,1,512]{2,1,0:T(1,128)S(1)}, f32[4,1,512]{2,1,0:T(1,128)S(1)}, u32[]{:S(2)}, u32[]{:S(2)}) collective-permute-start(f32[4,1,512]{2,1,0:T(1,128)S(1)} %get-tuple-element.92), channel_id=1, source_target_pairs={{8,0},{16,8},{24,16},{9,1},{17,9},{25,17},{10,2},{18,10},{26,18},{... | collective-permute-start | bytes 24584 | tf_op jit(solution)/shard_map/while/body/eval_jaxpr/ppermute | solution.py:34
  213.5 5.9 %collective-permute-start.1 = (f32[4,1,512]{2,1,0:T(1,128)S(1)}, f32[4,1,512]{2,1,0:T(1,128)S(1)}, u32[]{:S(2)}, u32[]{:S(2)}) collective-permute-start(f32[4,1,512]{2,1,0:T(1,128)S(1)} %get-tuple-element.93), channel_id=1, source_target_pairs={{0,8},{8,16},{16,24},{1,9},{9,17},{17,25},{2,10},{10,18},{18,26},{... | collective-permute-start | bytes 24584 | tf_op jit(solution)/shard_map/while/body/eval_jaxpr/ppermute | solution.py:33
  219.5 8.0 %collective-permute-start.2 = (f32[4,34,1]{2,1,0:T(8,128)S(1)}, f32[4,34,1]{2,1,0:T(8,128)S(1)}, u32[]{:S(2)}, u32[]{:S(2)}) collective-permute-start(f32[4,34,1]{2,1,0:T(8,128)S(1)} %get-tuple-element.94), channel_id=1, source_target_pairs={{1,0},{2,1},{3,2},{4,3},{5,4},{6,5},{7,6},{9,8},{10,9},{11,10},{12... | collective-permute-start | bytes 1640 | tf_op jit(solution)/shard_map/while/body/eval_jaxpr/ppermute | solution.py:34
  220.8 7.6 %collective-permute-start.3 = (f32[4,34,1]{2,1,0:T(8,128)S(1)}, f32[4,34,1]{2,1,0:T(8,128)S(1)}, u32[]{:S(2)}, u32[]{:S(2)}) collective-permute-start(f32[4,34,1]{2,1,0:T(8,128)S(1)} %get-tuple-element.95), channel_id=1, source_target_pairs={{0,1},{1,2},{2,3},{3,4},{4,5},{5,6},{6,7},{8,9},{9,10},{10,11},{11... | collective-permute-start | bytes 1640 | tf_op jit(solution)/shard_map/while/body/eval_jaxpr/ppermute | solution.py:33
  230.4 5.9 %collective-permute-start.1 = (f32[4,1,512]{2,1,0:T(1,128)S(1)}, f32[4,1,512]{2,1,0:T(1,128)S(1)}, u32[]{:S(2)}, u32[]{:S(2)}) collective-permute-start(f32[4,1,512]{2,1,0:T(1,128)S(1)} %get-tuple-element.93), channel_id=1, source_target_pairs={{0,8},{8,16},{16,24},{1,9},{9,17},{17,25},{2,10},{10,18},{18,26},{... | collective-permute-start | bytes 24584 | tf_op jit(solution)/shard_map/while/body/eval_jaxpr/ppermute | solution.py:33
  236.4 8.0 %collective-permute-start.2 = (f32[4,34,1]{2,1,0:T(8,128)S(1)}, f32[4,34,1]{2,1,0:T(8,128)S(1)}, u32[]{:S(2)}, u32[]{:S(2)}) collective-permute-start(f32[4,34,1]{2,1,0:T(8,128)S(1)} %get-tuple-element.94), channel_id=1, source_target_pairs={{1,0},{2,1},{3,2},{4,3},{5,4},{6,5},{7,6},{9,8},{10,9},{11,10},{12... | collective-permute-start | bytes 1640 | tf_op jit(solution)/shard_map/while/body/eval_jaxpr/ppermute | solution.py:34
  237.7 7.6 %collective-permute-start.3 = (f32[4,34,1]{2,1,0:T(8,128)S(1)}, f32[4,34,1]{2,1,0:T(8,128)S(1)}, u32[]{:S(2)}, u32[]{:S(2)}) collective-permute-start(f32[4,34,1]{2,1,0:T(8,128)S(1)} %get-tuple-element.95), channel_id=1, source_target_pairs={{0,1},{1,2},{2,3},{3,4},{4,5},{5,6},{6,7},{8,9},{9,10},{10,11},{11... | collective-permute-start | bytes 1640 | tf_op jit(solution)/shard_map/while/body/eval_jaxpr/ppermute | solution.py:33
  246.0 5.9 %collective-permute-start = (f32[4,1,512]{2,1,0:T(1,128)S(1)}, f32[4,1,512]{2,1,0:T(1,128)S(1)}, u32[]{:S(2)}, u32[]{:S(2)}) collective-permute-start(f32[4,1,512]{2,1,0:T(1,128)S(1)} %get-tuple-element.92), channel_id=1, source_target_pairs={{8,0},{16,8},{24,16},{9,1},{17,9},{25,17},{10,2},{18,10},{26,18},{... | collective-permute-start | bytes 24584 | tf_op jit(solution)/shard_map/while/body/eval_jaxpr/ppermute | solution.py:34
  247.3 5.9 %collective-permute-start.1 = (f32[4,1,512]{2,1,0:T(1,128)S(1)}, f32[4,1,512]{2,1,0:T(1,128)S(1)}, u32[]{:S(2)}, u32[]{:S(2)}) collective-permute-start(f32[4,1,512]{2,1,0:T(1,128)S(1)} %get-tuple-element.93), channel_id=1, source_target_pairs={{0,8},{8,16},{16,24},{1,9},{9,17},{17,25},{2,10},{10,18},{18,26},{... | collective-permute-start | bytes 24584 | tf_op jit(solution)/shard_map/while/body/eval_jaxpr/ppermute | solution.py:33
  253.3 8.0 %collective-permute-start.2 = (f32[4,34,1]{2,1,0:T(8,128)S(1)}, f32[4,34,1]{2,1,0:T(8,128)S(1)}, u32[]{:S(2)}, u32[]{:S(2)}) collective-permute-start(f32[4,34,1]{2,1,0:T(8,128)S(1)} %get-tuple-element.94), channel_id=1, source_target_pairs={{1,0},{2,1},{3,2},{4,3},{5,4},{6,5},{7,6},{9,8},{10,9},{11,10},{12... | collective-permute-start | bytes 1640 | tf_op jit(solution)/shard_map/while/body/eval_jaxpr/ppermute | solution.py:34
  254.6 7.6 %collective-permute-start.3 = (f32[4,34,1]{2,1,0:T(8,128)S(1)}, f32[4,34,1]{2,1,0:T(8,128)S(1)}, u32[]{:S(2)}, u32[]{:S(2)}) collective-permute-start(f32[4,34,1]{2,1,0:T(8,128)S(1)} %get-tuple-element.95), channel_id=1, source_target_pairs={{0,1},{1,2},{2,3},{3,4},{4,5},{5,6},{6,7},{8,9},{9,10},{10,11},{11... | collective-permute-start | bytes 1640 | tf_op jit(solution)/shard_map/while/body/eval_jaxpr/ppermute | solution.py:33
  264.2 5.9 %collective-permute-start.1 = (f32[4,1,512]{2,1,0:T(1,128)S(1)}, f32[4,1,512]{2,1,0:T(1,128)S(1)}, u32[]{:S(2)}, u32[]{:S(2)}) collective-permute-start(f32[4,1,512]{2,1,0:T(1,128)S(1)} %get-tuple-element.93), channel_id=1, source_target_pairs={{0,8},{8,16},{16,24},{1,9},{9,17},{17,25},{2,10},{10,18},{18,26},{... | collective-permute-start | bytes 24584 | tf_op jit(solution)/shard_map/while/body/eval_jaxpr/ppermute | solution.py:33
  270.2 8.0 %collective-permute-start.2 = (f32[4,34,1]{2,1,0:T(8,128)S(1)}, f32[4,34,1]{2,1,0:T(8,128)S(1)}, u32[]{:S(2)}, u32[]{:S(2)}) collective-permute-start(f32[4,34,1]{2,1,0:T(8,128)S(1)} %get-tuple-element.94), channel_id=1, source_target_pairs={{1,0},{2,1},{3,2},{4,3},{5,4},{6,5},{7,6},{9,8},{10,9},{11,10},{12... | collective-permute-start | bytes 1640 | tf_op jit(solution)/shard_map/while/body/eval_jaxpr/ppermute | solution.py:34
  271.5 7.6 %collective-permute-start.3 = (f32[4,34,1]{2,1,0:T(8,128)S(1)}, f32[4,34,1]{2,1,0:T(8,128)S(1)}, u32[]{:S(2)}, u32[]{:S(2)}) collective-permute-start(f32[4,34,1]{2,1,0:T(8,128)S(1)} %get-tuple-element.95), channel_id=1, source_target_pairs={{0,1},{1,2},{2,3},{3,4},{4,5},{5,6},{6,7},{8,9},{9,10},{10,11},{11... | collective-permute-start | bytes 1640 | tf_op jit(solution)/shard_map/while/body/eval_jaxpr/ppermute | solution.py:33
  281.1 5.9 %collective-permute-start.1 = (f32[4,1,512]{2,1,0:T(1,128)S(1)}, f32[4,1,512]{2,1,0:T(1,128)S(1)}, u32[]{:S(2)}, u32[]{:S(2)}) collective-permute-start(f32[4,1,512]{2,1,0:T(1,128)S(1)} %get-tuple-element.93), channel_id=1, source_target_pairs={{0,8},{8,16},{16,24},{1,9},{9,17},{17,25},{2,10},{10,18},{18,26},{... | collective-permute-start | bytes 24584 | tf_op jit(solution)/shard_map/while/body/eval_jaxpr/ppermute | solution.py:33
  287.1 8.0 %collective-permute-start.2 = (f32[4,34,1]{2,1,0:T(8,128)S(1)}, f32[4,34,1]{2,1,0:T(8,128)S(1)}, u32[]{:S(2)}, u32[]{:S(2)}) collective-permute-start(f32[4,34,1]{2,1,0:T(8,128)S(1)} %get-tuple-element.94), channel_id=1, source_target_pairs={{1,0},{2,1},{3,2},{4,3},{5,4},{6,5},{7,6},{9,8},{10,9},{11,10},{12... | collective-permute-start | bytes 1640 | tf_op jit(solution)/shard_map/while/body/eval_jaxpr/ppermute | solution.py:34
  288.4 7.6 %collective-permute-start.3 = (f32[4,34,1]{2,1,0:T(8,128)S(1)}, f32[4,34,1]{2,1,0:T(8,128)S(1)}, u32[]{:S(2)}, u32[]{:S(2)}) collective-permute-start(f32[4,34,1]{2,1,0:T(8,128)S(1)} %get-tuple-element.95), channel_id=1, source_target_pairs={{0,1},{1,2},{2,3},{3,4},{4,5},{5,6},{6,7},{8,9},{9,10},{10,11},{11... | collective-permute-start | bytes 1640 | tf_op jit(solution)/shard_map/while/body/eval_jaxpr/ppermute | solution.py:33
  298.0 5.9 %collective-permute-start.1 = (f32[4,1,512]{2,1,0:T(1,128)S(1)}, f32[4,1,512]{2,1,0:T(1,128)S(1)}, u32[]{:S(2)}, u32[]{:S(2)}) collective-permute-start(f32[4,1,512]{2,1,0:T(1,128)S(1)} %get-tuple-element.93), channel_id=1, source_target_pairs={{0,8},{8,16},{16,24},{1,9},{9,17},{17,25},{2,10},{10,18},{18,26},{... | collective-permute-start | bytes 24584 | tf_op jit(solution)/shard_map/while/body/eval_jaxpr/ppermute | solution.py:33
  304.0 8.0 %collective-permute-start.2 = (f32[4,34,1]{2,1,0:T(8,128)S(1)}, f32[4,34,1]{2,1,0:T(8,128)S(1)}, u32[]{:S(2)}, u32[]{:S(2)}) collective-permute-start(f32[4,34,1]{2,1,0:T(8,128)S(1)} %get-tuple-element.94), channel_id=1, source_target_pairs={{1,0},{2,1},{3,2},{4,3},{5,4},{6,5},{7,6},{9,8},{10,9},{11,10},{12... | collective-permute-start | bytes 1640 | tf_op jit(solution)/shard_map/while/body/eval_jaxpr/ppermute | solution.py:34
  305.3 7.6 %collective-permute-start.3 = (f32[4,34,1]{2,1,0:T(8,128)S(1)}, f32[4,34,1]{2,1,0:T(8,128)S(1)}, u32[]{:S(2)}, u32[]{:S(2)}) collective-permute-start(f32[4,34,1]{2,1,0:T(8,128)S(1)} %get-tuple-element.95), channel_id=1, source_target_pairs={{0,1},{1,2},{2,3},{3,4},{4,5},{5,6},{6,7},{8,9},{9,10},{10,11},{11... | collective-permute-start | bytes 1640 | tf_op jit(solution)/shard_map/while/body/eval_jaxpr/ppermute | solution.py:33
  314.9 5.9 %collective-permute-start.1 = (f32[4,1,512]{2,1,0:T(1,128)S(1)}, f32[4,1,512]{2,1,0:T(1,128)S(1)}, u32[]{:S(2)}, u32[]{:S(2)}) collective-permute-start(f32[4,1,512]{2,1,0:T(1,128)S(1)} %get-tuple-element.93), channel_id=1, source_target_pairs={{0,8},{8,16},{16,24},{1,9},{9,17},{17,25},{2,10},{10,18},{18,26},{... | collective-permute-start | bytes 24584 | tf_op jit(solution)/shard_map/while/body/eval_jaxpr/ppermute | solution.py:33
  320.9 8.0 %collective-permute-start.2 = (f32[4,34,1]{2,1,0:T(8,128)S(1)}, f32[4,34,1]{2,1,0:T(8,128)S(1)}, u32[]{:S(2)}, u32[]{:S(2)}) collective-permute-start(f32[4,34,1]{2,1,0:T(8,128)S(1)} %get-tuple-element.94), channel_id=1, source_target_pairs={{1,0},{2,1},{3,2},{4,3},{5,4},{6,5},{7,6},{9,8},{10,9},{11,10},{12... | collective-permute-start | bytes 1640 | tf_op jit(solution)/shard_map/while/body/eval_jaxpr/ppermute | solution.py:34
  322.2 7.6 %collective-permute-start.3 = (f32[4,34,1]{2,1,0:T(8,128)S(1)}, f32[4,34,1]{2,1,0:T(8,128)S(1)}, u32[]{:S(2)}, u32[]{:S(2)}) collective-permute-start(f32[4,34,1]{2,1,0:T(8,128)S(1)} %get-tuple-element.95), channel_id=1, source_target_pairs={{0,1},{1,2},{2,3},{3,4},{4,5},{5,6},{6,7},{8,9},{9,10},{10,11},{11... | collective-permute-start | bytes 1640 | tf_op jit(solution)/shard_map/while/body/eval_jaxpr/ppermute | solution.py:33
  331.8 5.9 %collective-permute-start.1 = (f32[4,1,512]{2,1,0:T(1,128)S(1)}, f32[4,1,512]{2,1,0:T(1,128)S(1)}, u32[]{:S(2)}, u32[]{:S(2)}) collective-permute-start(f32[4,1,512]{2,1,0:T(1,128)S(1)} %get-tuple-element.93), channel_id=1, source_target_pairs={{0,8},{8,16},{16,24},{1,9},{9,17},{17,25},{2,10},{10,18},{18,26},{... | collective-permute-start | bytes 24584 | tf_op jit(solution)/shard_map/while/body/eval_jaxpr/ppermute | solution.py:33
  337.8 8.0 %collective-permute-start.2 = (f32[4,34,1]{2,1,0:T(8,128)S(1)}, f32[4,34,1]{2,1,0:T(8,128)S(1)}, u32[]{:S(2)}, u32[]{:S(2)}) collective-permute-start(f32[4,34,1]{2,1,0:T(8,128)S(1)} %get-tuple-element.94), channel_id=1, source_target_pairs={{1,0},{2,1},{3,2},{4,3},{5,4},{6,5},{7,6},{9,8},{10,9},{11,10},{12... | collective-permute-start | bytes 1640 | tf_op jit(solution)/shard_map/while/body/eval_jaxpr/ppermute | solution.py:34
  339.1 7.6 %collective-permute-start.3 = (f32[4,34,1]{2,1,0:T(8,128)S(1)}, f32[4,34,1]{2,1,0:T(8,128)S(1)}, u32[]{:S(2)}, u32[]{:S(2)}) collective-permute-start(f32[4,34,1]{2,1,0:T(8,128)S(1)} %get-tuple-element.95), channel_id=1, source_target_pairs={{0,1},{1,2},{2,3},{3,4},{4,5},{5,6},{6,7},{8,9},{9,10},{10,11},{11... | collective-permute-start | bytes 1640 | tf_op jit(solution)/shard_map/while/body/eval_jaxpr/ppermute | solution.py:33
  348.7 5.9 %collective-permute-start.1 = (f32[4,1,512]{2,1,0:T(1,128)S(1)}, f32[4,1,512]{2,1,0:T(1,128)S(1)}, u32[]{:S(2)}, u32[]{:S(2)}) collective-permute-start(f32[4,1,512]{2,1,0:T(1,128)S(1)} %get-tuple-element.93), channel_id=1, source_target_pairs={{0,8},{8,16},{16,24},{1,9},{9,17},{17,25},{2,10},{10,18},{18,26},{... | collective-permute-start | bytes 24584 | tf_op jit(solution)/shard_map/while/body/eval_jaxpr/ppermute | solution.py:33
  354.7 8.0 %collective-permute-start.2 = (f32[4,34,1]{2,1,0:T(8,128)S(1)}, f32[4,34,1]{2,1,0:T(8,128)S(1)}, u32[]{:S(2)}, u32[]{:S(2)}) collective-permute-start(f32[4,34,1]{2,1,0:T(8,128)S(1)} %get-tuple-element.94), channel_id=1, source_target_pairs={{1,0},{2,1},{3,2},{4,3},{5,4},{6,5},{7,6},{9,8},{10,9},{11,10},{12... | collective-permute-start | bytes 1640 | tf_op jit(solution)/shard_map/while/body/eval_jaxpr/ppermute | solution.py:34
  356.0 7.6 %collective-permute-start.3 = (f32[4,34,1]{2,1,0:T(8,128)S(1)}, f32[4,34,1]{2,1,0:T(8,128)S(1)}, u32[]{:S(2)}, u32[]{:S(2)}) collective-permute-start(f32[4,34,1]{2,1,0:T(8,128)S(1)} %get-tuple-element.95), channel_id=1, source_target_pairs={{0,1},{1,2},{2,3},{3,4},{4,5},{5,6},{6,7},{8,9},{9,10},{10,11},{11... | collective-permute-start | bytes 1640 | tf_op jit(solution)/shard_map/while/body/eval_jaxpr/ppermute | solution.py:33
  365.6 5.9 %collective-permute-start.1 = (f32[4,1,512]{2,1,0:T(1,128)S(1)}, f32[4,1,512]{2,1,0:T(1,128)S(1)}, u32[]{:S(2)}, u32[]{:S(2)}) collective-permute-start(f32[4,1,512]{2,1,0:T(1,128)S(1)} %get-tuple-element.93), channel_id=1, source_target_pairs={{0,8},{8,16},{16,24},{1,9},{9,17},{17,25},{2,10},{10,18},{18,26},{... | collective-permute-start | bytes 24584 | tf_op jit(solution)/shard_map/while/body/eval_jaxpr/ppermute | solution.py:33
  371.6 8.0 %collective-permute-start.2 = (f32[4,34,1]{2,1,0:T(8,128)S(1)}, f32[4,34,1]{2,1,0:T(8,128)S(1)}, u32[]{:S(2)}, u32[]{:S(2)}) collective-permute-start(f32[4,34,1]{2,1,0:T(8,128)S(1)} %get-tuple-element.94), channel_id=1, source_target_pairs={{1,0},{2,1},{3,2},{4,3},{5,4},{6,5},{7,6},{9,8},{10,9},{11,10},{12... | collective-permute-start | bytes 1640 | tf_op jit(solution)/shard_map/while/body/eval_jaxpr/ppermute | solution.py:34
  372.9 7.6 %collective-permute-start.3 = (f32[4,34,1]{2,1,0:T(8,128)S(1)}, f32[4,34,1]{2,1,0:T(8,128)S(1)}, u32[]{:S(2)}, u32[]{:S(2)}) collective-permute-start(f32[4,34,1]{2,1,0:T(8,128)S(1)} %get-tuple-element.95), channel_id=1, source_target_pairs={{0,1},{1,2},{2,3},{3,4},{4,5},{5,6},{6,7},{8,9},{9,10},{10,11},{11... | collective-permute-start | bytes 1640 | tf_op jit(solution)/shard_map/while/body/eval_jaxpr/ppermute | solution.py:33
  405.8 22.7 %all-to-all-start = ((f32[8,16,512]{2,1,0:T(8,128)}), f32[8,16,512]{2,1,0:T(8,128)S(1)}, u32[]{:S(2)}, u32[]{:S(2)}) async-start(f32[8,16,512]{2,1,0:T(8,128)} %bitcast.26), calls=%async_computation | async-start | bytes 524288 | tf_op jit(solution)/shard_map/all_to_all | solution.py:165
  (24 other events, 164.7 us)
where the time goes:
time: 440 us; the launch traced here: 438 us
  starting transfers between devices  277 us (63%)
  waiting for transfers between devices  47.7 us (11%)
  other arithmetic  46.8 us (11%)
  local copies, waits for them, and re-layouts  29.3 us (7%)
  blocking collectives  19.7 us (4%)
  matrix products  14.3 us (3%)
    ppermute x40, starting transfers between devices, padded_2(): before = lax.ppermute(last, axis, up)  210 us
    ppermute x40, starting transfers between devices, padded_2(): after = lax.ppermute(first, axis, down)  51.7 us
    ppermute x40, waiting for transfers between devices, padded_2(): before = lax.ppermute(last, axis, up)  44.6 us
    scatter-add x1, other arithmetic, body(): counts = jnp.zeros((OX * WTAB, tile_count * ABLK), jnp.float32).at[group_...  25.9 us
    scatter x1, local copies, waits for them, and re-layouts, body(): return_rows = jnp.zeros((tile_count, capacity), jnp.int32).at[sender, slo...  22.1 us
    all_to_all x1, starting transfers between devices, body(): lax.all_to_all(outgoing_surface, 'tile', split_axis=0, concat_axis=0, til...  15.8 us
    all_gather x1, blocking collectives, body(): lax.all_gather(blocks, 'tile', axis=0, tiled=True)  10.8 us
    all_gather x1, blocking collectives, body(): lax.all_gather(overlay_pairings.astype(jnp.float32), 'tile', axis=1, tile...  8.88 us
  transfers between devices with their start and end apart: 81, of which 41 were waited for; matrix products, arithmetic and copies ran while one was open for 1% of the time, Pallas kernels for 0%

commit v1 on v0

v1 whole, which is shorter than its diff:
```python
import functools
import jax
import jax.numpy as jnp
from jax import lax
from jax.experimental import pallas as pl
from jax.experimental.pallas import tpu as pltpu
from jax.sharding import PartitionSpec as P

VERTICAL_LAYERS = 48
F = 4
BA = 256
ABLK = 8
WTAB = 8
OX = 32
BO = 512
SUB = 20
HALO = 24
ROWS = OX + 2 * HALO
LANES = 128
WIDE = BO + LANES

wave_speed = 0.25
mixing = 0.15
rotation = 0.1
tracer_mixing = 0.2
forcing_rate = 0.05
transfer_constant = 0.5
dewpoint_moisture_limit = 0.6

MESH = pl.DeviceIdType.MESH
DIRECTIONS = [(dc, dt) for dc in (-1, 0, 1) for dt in (-1, 0, 1) if (dc, dt) != (0, 0)]
FIELDS_MASK = (0, 5)
FORCING = (5, 9)

NT = (((1,), (1,)), ((), ()))
NN = (((1,), (0,)), ((), ()))


def mm(a, b, dims):
    return lax.dot_general(a, b, dims, preferred_element_type=jnp.float32)


def split(x):
    high = x.astype(jnp.bfloat16)
    return high, (x - high.astype(jnp.float32)).astype(jnp.bfloat16)


def stencil_rows(x_ref, first, last):
    sub = lax.broadcasted_iota(jnp.int32, (8, WIDE), 0)
    top, bottom = sub == 0, sub == 7

    def tile(row):
        return [x_ref[f, row:row + 8, :] for f in range(4)]

    before = tile(max(first - 8, 0))
    here = tile(first)
    for row in range(first, last, 8):
        after = tile(row + 8) if row + 8 < ROWS else here
        north = [pltpu.roll(jnp.where(top, a, h), 7, 0) for a, h in zip(after, here)]
        south = [pltpu.roll(jnp.where(bottom, b, h), 1, 0) for b, h in zip(before, here)]
        east = [pltpu.roll(h, WIDE - 1, 1) for h in here]
        west = [pltpu.roll(h, 1, 1) for h in here]
        around = [(n + s) + (e + w) for n, s, e, w in zip(north, south, east, west)]
        mask = x_ref[4, row:row + 8, :]
        forced = [x_ref[5 + f, row:row + 8, :] for f in range(4)]
        half = 0.5 * wave_speed
        keep = 1.0 - 4.0 * mixing
        eta, u, v, t = here
        new = [
            keep * eta + mixing * around[0]
            - half * ((east[1] - west[1]) + (north[2] - south[2])) + forced[1],
            keep * u + mixing * around[1] - half * (east[0] - west[0])
            + rotation * v + forced[2],
            keep * v + mixing * around[2] - half * (north[0] - south[0])
            - rotation * u + forced[3],
            (1.0 - 4.0 * tracer_mixing) * t + tracer_mixing * around[3] + forced[0],
        ]
        for f in range(4):
            x_ref[f, row:row + 8, :] = new[f] * mask
        before, here = here, after


def kernel(nc, nt, flux_ref, list_ref, w_hbm, fields_ref, mask_ref, out_ref, sst_ref,
           flux_all, list_all, w_ref, w_hi, w_lo, x_ref, side_ref, counts, counts_t, lhs,
           z_ref, part_out, part_in, denom,
           w_sem, flux_send, flux_recv, list_send, list_recv, part_send, part_recv,
           halo_send, halo_recv):
    comp, tile = lax.axis_index("comp"), lax.axis_index("tile")
    w_copy = pltpu.make_async_copy(w_hbm, w_ref, w_sem)
    w_copy.start()

    def inside(dc, dt):
        ok = None
        for pos, step, size in ((comp, dc, nc), (tile, dt, nt)):
            here = None
            if step > 0:
                here = pos + step < size
            if step < 0:
                here = pos + step >= 0
            if here is not None:
                ok = here if ok is None else jnp.logical_and(ok, here)
        return ok

    x_ref[:, 0:HALO, :] = jnp.zeros((9, HALO, WIDE), jnp.float32)
    x_ref[:, HALO + OX:ROWS, :] = jnp.zeros((9, HALO, WIDE), jnp.float32)
    side_ref[...] = jnp.zeros_like(side_ref)
    x_ref[0:4, HALO:HALO + OX, 0:BO] = fields_ref[...]
    x_ref[4, HALO:HALO + OX, 0:BO] = mask_ref[...].astype(jnp.float32)
    flux_all[tile] = flux_ref[...]
    list_all[tile] = list_ref[...]

    barrier = pltpu.get_barrier_semaphore()

    def greet(d, carry):
        pl.semaphore_signal(
            barrier, inc=1, device_id=(comp, lax.rem(tile + d, nt)), device_id_type=MESH
        )
        return carry

    lax.fori_loop(1, nt, greet, 0)
    far = [d for d in DIRECTIONS if d[0] != 0]
    for dc, dt in far:
        @pl.when(inside(dc, dt))
        def _():
            pl.semaphore_signal(
                barrier, inc=1, device_id=(comp + dc, tile + dt), device_id_type=MESH
            )
    beside = [
        jnp.minimum(pos, 1) + jnp.minimum(size - 1 - pos, 1)
        for pos, size in ((comp, nc), (tile, nt))
    ]
    pl.semaphore_wait(barrier, nt - 1 + beside[0] * (1 + beside[1]))

    def peer_copy(src, dst, send, recv, d):
        return pltpu.make_async_remote_copy(
            src_ref=src, dst_ref=dst, send_sem=send.at[d], recv_sem=recv.at[d],
            device_id=(comp, lax.rem(tile + d, nt)), device_id_type=MESH,
        )

    def list_copy(d):
        return peer_copy(list_ref, list_all.at[tile], list_send, list_recv, d)

    def flux_copy(d):
        return peer_copy(flux_ref, flux_all.at[tile], flux_send, flux_recv, d)

    def part_copy(d):
        return peer_copy(
            part_out.at[lax.rem(tile + d, nt)], part_in.at[tile], part_send, part_recv, d
        )

    def each_peer(action):
        def step(d, carry):
            action(d)
            return carry
        lax.fori_loop(1, nt, step, 0)

    each_peer(lambda d: list_copy(d).start())
    each_peer(lambda d: flux_copy(d).start())

    def halo_copy(phase, number):
        dc, dt = DIRECTIONS[number]
        low, high = FIELDS_MASK if phase == 0 else FORCING
        planes = pl.ds(low, high - low)
        if dc == 0:
            src_rows, dst_rows = pl.ds(HALO, OX), pl.ds(HALO, OX)
        elif dc > 0:
            src_rows, dst_rows = pl.ds(OX, HALO), pl.ds(0, HALO)
        else:
            src_rows, dst_rows = pl.ds(HALO, HALO), pl.ds(HALO + OX, HALO)
        if dt == 0:
            src = x_ref.at[planes, src_rows, pl.ds(0, BO)]
            dst = x_ref.at[planes, dst_rows, pl.ds(0, BO)]
        elif dt > 0:
            src = x_ref.at[planes, src_rows, pl.ds(BO - LANES, LANES)]
            dst = side_ref.at[0, planes, dst_rows, :]
        else:
            src = x_ref.at[planes, src_rows, pl.ds(0, LANES)]
            dst = side_ref.at[1, planes, dst_rows, :]
        return pltpu.make_async_remote_copy(
            src_ref=src, dst_ref=dst,
            send_sem=halo_send.at[phase, number], recv_sem=halo_recv.at[phase, number],
            device_id=(comp + dc, tile + dt), device_id_type=MESH,
        )

    def halo_start(phase):
        for number, (dc, dt) in enumerate(DIRECTIONS):
            @pl.when(inside(dc, dt))
            def _():
                halo_copy(phase, number).start()

    def halo_wait(phase):
        for number, (dc, dt) in enumerate(DIRECTIONS):
            @pl.when(inside(dc, dt))
            def _():
                halo_copy(phase, number).wait_send()

            @pl.when(inside(-dc, -dt))
            def _():
                halo_copy(phase, number).wait_recv()

    halo_start(0)

    mine = list_ref[...]
    row8 = lax.broadcasted_iota(jnp.int32, (8, LANES), 0)
    own_block = (row8 == mine[0:1, :]).astype(jnp.bfloat16)
    own_weight = (row8 == mine[3:4, :]).astype(jnp.bfloat16)
    named = mm(own_block, own_weight, NT)
    ones = jnp.ones((16, BO), jnp.bfloat16)
    w_copy.wait()
    total = jnp.zeros((ABLK, BA), jnp.float32)
    for w in range(WTAB):
        high, low = split(w_ref[w])
        w_hi[w] = high
        w_lo[w] = low
        sums = mm(ones, high, NT) + mm(ones, low, NT)
        total = total + named[:, w:w + 1] * sums[0:ABLK, :]
    denom[...] = total

    each_peer(lambda d: list_copy(d).wait())
    counts[...] = jnp.zeros_like(counts)
    counts_t[...] = jnp.zeros_like(counts_t)

    def count(source, carry):
        listing = list_all[source]
        code = jnp.where(listing[1:2, :] == tile, listing[3:4, :] * OX + listing[2:3, :], -1)
        group = lax.broadcasted_iota(jnp.int32, (WTAB * OX, LANES), 0) == code
        block = lax.broadcasted_iota(jnp.int32, (nt * ABLK, LANES), 0) == (
            jnp.where(listing[0:1, :] >= 0, source * ABLK + listing[0:1, :], -1)
        )
        group, block = group.astype(jnp.bfloat16), block.astype(jnp.bfloat16)
        counts[...] += mm(group, block, NT)
        counts_t[...] += mm(block, group, NT)
        return carry

    lax.fori_loop(0, nt, count, 0)
    count_fw = counts[...].astype(jnp.bfloat16)

    each_peer(lambda d: flux_copy(d).wait())
    for f in range(F):
        high, low = split(flux_all[:, f].reshape(nt * ABLK, BA))
        grouped = mm(count_fw, high, NN) + mm(count_fw, low, NN)
        high, low = split(grouped)
        for w in range(WTAB):
            lhs[w, f * OX:(f + 1) * OX, :] = high[w * OX:(w + 1) * OX]
            lhs[w, (F + f) * OX:(F + f + 1) * OX, :] = low[w * OX:(w + 1) * OX]
    half = F * OX
    acc = jnp.zeros((half, BO), jnp.float32)
    for w in range(WTAB):
        both = mm(lhs[w], w_hi[w], NN)
        acc = acc + ((both[half:] + mm(lhs[w, 0:half, :], w_lo[w], NN)) + both[:half])
    acc = acc * forcing_rate
    for f in range(F):
        x_ref[5 + f, HALO:HALO + OX, 0:BO] = acc[f * OX:(f + 1) * OX]
    halo_start(1)
    halo_wait(0)
    halo_wait(1)

    lane = lax.broadcasted_iota(jnp.int32, (ROWS, LANES), 1)
    for k in range(9):
        x_ref[k, :, BO:WIDE] = jnp.where(lane < LANES // 2, side_ref[1, k], side_ref[0, k])

    done = 0
    while done < SUB:
        def window(step):
            depth = SUB - step
            return (HALO - depth) // 8 * 8, -(-(HALO + OX + depth) // 8) * 8
        first, last = window(done + 1)
        upto = done + 1
        while upto < SUB and window(upto + 1) == (first, last):
            upto += 1

        def substep(i, carry):
            stencil_rows(x_ref, first, last)
            return carry

        lax.fori_loop(0, upto - done, substep, 0)
        done = upto

    out_ref[...] = x_ref[0:4, HALO:HALO + OX, 0:BO]
    high, low = split(x_ref[3, HALO:HALO + OX, 0:BO])
    both = jnp.concatenate([high, low], axis=0)
    for w in range(WTAB):
        product = mm(both, w_hi[w], NT)
        z_ref[w * OX:(w + 1) * OX, :] = product[:OX] + (product[OX:] + mm(high, w_lo[w], NT))
    count_bw = counts_t[...].astype(jnp.bfloat16)
    high, low = split(z_ref[...])
    partial = mm(count_bw, high, NN) + mm(count_bw, low, NN)
    part_out[...] = partial.reshape(nt, ABLK, BA)
    each_peer(lambda d: part_copy(d).start())
    part_in[tile] = part_out[tile]
    each_peer(lambda d: part_copy(d).wait())
    sst_ref[...] = jnp.sum(part_in[...], axis=0) / denom[...]


def body(nc, nt, columns, solver, warmth, weights, pairings, fields, indicator):
    renewed = jnp.dot(
        solver, columns, precision=lax.Precision.HIGHEST, preferred_element_type=jnp.float32
    )
    air, moisture, wind_east, wind_north = (
        renewed[k * VERTICAL_LAYERS - 1] for k in (1, 2, 3, 4)
    )
    speed = transfer_constant * jnp.sqrt(wind_east * wind_east + wind_north * wind_north + 1.0)
    flux = jnp.stack([
        speed * (warmth - air),
        speed * (dewpoint_moisture_limit * warmth - moisture),
        speed * wind_east,
        speed * wind_north,
    ]).reshape(F, ABLK, BA)
    listing = jnp.stack([
        pairings[0] // nt, pairings[1] // OX, pairings[1] % OX, pairings[2]
    ])
    listing = jnp.pad(
        listing, ((0, 8 - 4), (0, LANES - listing.shape[1])), constant_values=-1
    )
    vmem = pl.BlockSpec(memory_space=pltpu.VMEM)
    f32, bf16 = jnp.float32, jnp.bfloat16
    dma = pltpu.SemaphoreType.DMA
    stepped, regridded = pl.pallas_call(
        functools.partial(kernel, nc, nt),
        out_shape=(
            jax.ShapeDtypeStruct((4, OX, BO), f32), jax.ShapeDtypeStruct((ABLK, BA), f32)
        ),
        in_specs=[vmem, vmem, pl.BlockSpec(memory_space=pl.ANY), vmem, vmem],
        out_specs=(vmem, vmem),
        scratch_shapes=[
            pltpu.VMEM((nt, F, ABLK, BA), f32),
            pltpu.VMEM((nt, 8, LANES), jnp.int32),
            pltpu.VMEM((WTAB, BA, BO), f32),
            pltpu.VMEM((WTAB, BA, BO), bf16),
            pltpu.VMEM((WTAB, BA, BO), bf16),
            pltpu.VMEM((9, ROWS, WIDE), f32),
            pltpu.VMEM((2, 9, ROWS, LANES), f32),
            pltpu.VMEM((WTAB * OX, nt * ABLK), f32),
            pltpu.VMEM((nt * ABLK, WTAB * OX), f32),
            pltpu.VMEM((WTAB, 2 * F * OX, BA), bf16),
            pltpu.VMEM((WTAB * OX, BA), f32),
            pltpu.VMEM((nt, ABLK, BA), f32),
            pltpu.VMEM((nt, ABLK, BA), f32),
            pltpu.VMEM((ABLK, BA), f32),
            dma,
            dma((nt,)), dma((nt,)), dma((nt,)), dma((nt,)), dma((nt,)), dma((nt,)),
            dma((2, 8)), dma((2, 8)),
        ],
        compiler_params=pltpu.CompilerParams(
            collective_id=0, has_side_effects=True, vmem_limit_bytes=48 * 1024 * 1024
        ),
        name="coupling",
    )(flux, listing, weights, fields, indicator)
    return renewed, stepped, regridded.reshape(-1)


def solution(mesh):
    placed = (
        P(None, ("comp", "tile")),
        P(),
        P(("comp", "tile")),
        P("comp", None, None),
        P(None, ("comp", "tile")),
        P(None, "comp", "tile"),
        P("comp", "tile"),
    )
    return jax.shard_map(
        functools.partial(body, mesh.shape["comp"], mesh.shape["tile"]),
        mesh=mesh,
        in_specs=placed,
        out_specs=(P(None, ("comp", "tile")), P(None, "comp", "tile"), P(("comp", "tile"))),
        check_vma=False,
    )
```

time: 440 us -> 44.6 us (0.10)
  starting transfers between devices: 277 us -> 0 us
  waiting for transfers between devices: 47.7 us -> 0 us
  other arithmetic: 46.8 us -> 0.96 us
  Pallas kernels: 0 us -> 35.8 us
  local copies, waits for them, and re-layouts: 29.3 us -> 4.45 us
  blocking collectives: 19.7 us -> 0 us
  matrix products: 14.3 us -> 2.42 us
    ppermute x80 -> x0, starting transfers between devices: 261 us -> none  [the longest x40 210 us: padded_2(): before = lax.ppermute(last, axis, up)]
    ppermute x80 -> x0, waiting for transfers between devices: 44.7 us -> none  [the longest x40 44.6 us: padded_2(): before = lax.ppermute(last, axis, up)]
    pallas_call x0 -> x1, Pallas kernels: none -> 35.8 us  [body(): pl.pallas_call(functools.partial(kernel, nc, nt), out_shape=(jax.ShapeDty...]
    scatter-add x3 -> x0, other arithmetic: 28.2 us -> none  [the longest x1 25.9 us: body(): counts = jnp.zeros((OX * WTAB, tile_count * ABLK), jnp.float32).at[group_...]
    scatter x1 -> x0, local copies, waits for them, and re-layouts: 22.1 us -> none  [body(): return_rows = jnp.zeros((tile_count, capacity), jnp.int32).at[sender, slo...]
    all_gather x2 -> x0, blocking collectives: 19.7 us -> none  [the longest x1 10.8 us: body(): lax.all_gather(blocks, 'tile', axis=0, tiled=True)]
    all_to_all x1 -> x0, starting transfers between devices: 15.8 us -> none  [body(): lax.all_to_all(outgoing_surface, 'tile', split_axis=0, concat_axis=0, til...]
    dot_general x4 -> x1, matrix products: 14.3 us -> 2.42 us  [body(): jnp.dot(solver, columns, precision=lax.Precision.HIGHEST, preferred_eleme...]
  transfers between devices with their start and end apart: 81 -> 0, of which waited for: 41 -> 0; matrix products, arithmetic and copies ran while one was open for 1% -> 0% of each run, Pallas kernels for 0% -> 0%
where the time goes in v1:
time: 44.6 us; the launch traced here: 44.4 us
  Pallas kernels  35.8 us (80%)
  local copies, waits for them, and re-layouts  4.45 us (10%)
  matrix products  2.42 us (5%)
  other arithmetic  0.96 us (2%)
  between operations  0.78 us (2%)
    pallas_call x1, Pallas kernels, body(): pl.pallas_call(functools.partial(kernel, nc, nt), out_shape=(jax.ShapeDty...  35.8 us
    unnamed x14, local copies, waits for them, and re-layouts  4.43 us
    dot_general x1, matrix products, body(): jnp.dot(solver, columns, precision=lax.Precision.HIGHEST, preferred_eleme...  2.42 us

profile of v1, /device:TPU:0, one launch (start us, length us, event | category | flops | bytes accessed | tf_op | source)
XLA Modules:
  0.0 44.4 jit_solution(6876907684273034124)
XLA Ops:
  0.6 0.0 copy-start
  0.6 0.8 %and_select_fusion.2 = (s32[1,64]{1,0:T(1,128)S(1)}, s32[1,64]{1,0:T(1,128)S(1)}, s32[1,64]{1,0:T(1,128)S(1)}, s32[1,64]{1,0:T(1,128)S(1)}) fusion(s32[3,64]{1,0:T(4,128)} %param.11), kind=kLoop, calls=%fused_computation.9 | loop fusion | flops 1920 | bytes 1792 | tf_op jit(solution)/shard_map/jit(floor_divide)/jit(_where)/select_n | solution.py:310
  1.5 0.6 %copy-done = f32[192,2048]{1,0:T(8,128)S(1)} copy-done((f32[192,2048]{1,0:T(8,128)S(1)}, f32[192,2048]{1,0:T(8,128)}, u32[]{:S(2)}) %copy-start) | copy-done | bytes 1572888
  2.1 0.0 copy-start.5
  2.1 0.0 copy-start.2
  2.1 0.0 copy-start.3
  2.1 2.4 %fusion.1 = f32[192,2048]{1,0:T(8,128)S(1)} fusion(f32[192,192]{1,0:T(8,128)} %param.8, f32[192,2048]{1,0:T(8,128)S(1)} %copy-done), kind=kOutput, calls=%fused_computation.17 | convolution fusion | flops 905969664 | bytes 3293184 | tf_op jit(solution)/shard_map/dot_general | solution.py:296
  4.5 0.0 copy-start.4
  4.5 0.1 fusion
  4.6 0.0 copy-done.5
  4.7 0.0 copy-done.2
  4.7 0.0 copy-done.3
  4.7 0.0 copy-start.1
  4.7 2.5 %copy-done.1 = f32[8,256,512]{2,1,0:T(8,128)S(1)} copy-done((f32[8,256,512]{2,1,0:T(8,128)S(1)}, f32[8,256,512]{2,1,0:T(8,128)}, u32[]{:S(2)}) %copy-start.1) | copy-done | bytes 4194328
  7.3 35.8 %coupling.1 = (f32[4,32,512]{2,1,0:T(8,128)S(1)}, f32[8,256]{1,0:T(8,128)S(1)}) custom-call(f32[4,8,256]{2,1,0:T(8,128)S(1)} %pad_maximum_fusion.flux_ref, s32[8,128]{1,0:T(8,128)S(1)} %pad.4.list_ref, f32[8,256,512]{2,1,0:T(8,128)S(1)} %copy-done.1, f32[4,32,512]{2,1,0:T(8,128)S(1)} %copy-done.2, s32[32,512]{1,0:T(8,128)S(1)} %copy-done.3), custom_call_target="tpu_custom_call" | custom-call | tf_op jit(solution)/shard_map/coupling/pallas_call | solution.py:318
  43.1 0.0 copy-done.4
  43.1 0.6 %copy.10 = f32[1,2,8,128]{3,1,2,0:T(2,128)} copy(f32[1,2,8,128]{3,2,1,0:T(8,128)S(1)} %bitcast.7) | data formatting | bytes 16384
  43.7 0.7 %copy.12 = f32[4,32,512]{2,1,0:T(8,128)} copy(f32[4,32,512]{2,1,0:T(8,128)S(1)} %get-tuple-element.27) | data formatting | bytes 524288
  (9 shorter events, 0.1 us)
Async XLA Ops:
  0.6 1.5 %copy-start = (f32[192,2048]{1,0:T(8,128)S(1)}, f32[192,2048]{1,0:T(8,128)}, u32[]{:S(2)}) copy-start(f32[192,2048]{1,0:T(8,128)} %param.7) | copy-start | bytes 4718596
  2.1 2.5 %copy-start.5 = (f32[2048]{0:T(1024)S(1)}, f32[2048]{0:T(1024)}, u32[]{:S(2)}) copy-start(f32[2048]{0:T(1024)} %param.9) | copy-start | bytes 24580
  2.1 2.6 %copy-start.2 = (f32[4,32,512]{2,1,0:T(8,128)S(1)}, f32[4,32,512]{2,1,0:T(8,128)}, u32[]{:S(2)}) copy-start(f32[4,32,512]{2,1,0:T(8,128)} %fields_ref.1) | copy-start | bytes 786436
  2.1 2.6 %copy-start.3 = (s32[32,512]{1,0:T(8,128)S(1)}, s32[32,512]{1,0:T(8,128)}, u32[]{:S(2)}) copy-start(s32[32,512]{1,0:T(8,128)} %mask_ref.1) | copy-start | bytes 196612
  4.5 38.5 %copy-start.4 = (f32[192,2048]{1,0:T(8,128)}, f32[192,2048]{1,0:T(8,128)S(1)}, u32[]{:S(2)}) copy-start(f32[192,2048]{1,0:T(8,128)S(1)} %fusion.1) | copy-start | bytes 4718596
  4.7 2.5 %copy-start.1 = (f32[8,256,512]{2,1,0:T(8,128)S(1)}, f32[8,256,512]{2,1,0:T(8,128)}, u32[]{:S(2)}) copy-start(f32[8,256,512]{2,1,0:T(8,128)} %w_hbm.1) | copy-start | bytes 12582916

commit v2 on v1

--- a/solution.py
+++ b/solution.py
@@ -28,9 +28,9 @@
 dewpoint_moisture_limit = 0.6
 
 MESH = pl.DeviceIdType.MESH
-DIRECTIONS = [(dc, dt) for dc in (-1, 0, 1) for dt in (-1, 0, 1) if (dc, dt) != (0, 0)]
-FIELDS_MASK = (0, 5)
-FORCING = (5, 9)
+DIRECTIONS = [(-1, 0), (1, 0), (-1, -1), (-1, 1), (1, -1), (1, 1), (0, -1), (0, 1)]
+STRIP = 32
+KINDS = [(0, 4), (4, 5), (5, 9)]
 
 NT = (((1,), (1,)), ((), ()))
 NN = (((1,), (0,)), ((), ()))
@@ -81,7 +81,7 @@
 
 
 def kernel(nc, nt, flux_ref, list_ref, w_hbm, fields_ref, mask_ref, out_ref, sst_ref,
-           flux_all, list_all, w_ref, w_hi, w_lo, x_ref, side_ref, counts, counts_t, lhs,
+           flux_all, list_all, w_ref, w_hi, w_lo, x_ref, side_ref, pack_ref, counts, counts_t, lhs,
            z_ref, part_out, part_in, denom,
            w_sem, flux_send, flux_recv, list_send, list_recv, part_send, part_recv,
            halo_send, halo_recv):
@@ -101,13 +101,9 @@
                 ok = here if ok is None else jnp.logical_and(ok, here)
         return ok
 
-    x_ref[:, 0:HALO, :] = jnp.zeros((9, HALO, WIDE), jnp.float32)
-    x_ref[:, HALO + OX:ROWS, :] = jnp.zeros((9, HALO, WIDE), jnp.float32)
+    x_ref[:, 0:HALO, 0:BO] = jnp.zeros((9, HALO, BO), jnp.float32)
+    x_ref[:, HALO + OX:ROWS, 0:BO] = jnp.zeros((9, HALO, BO), jnp.float32)
     side_ref[...] = jnp.zeros_like(side_ref)
-    x_ref[0:4, HALO:HALO + OX, 0:BO] = fields_ref[...]
-    x_ref[4, HALO:HALO + OX, 0:BO] = mask_ref[...].astype(jnp.float32)
-    flux_all[tile] = flux_ref[...]
-    list_all[tile] = list_ref[...]
 
     barrier = pltpu.get_barrier_semaphore()
 
@@ -125,6 +121,39 @@
             pl.semaphore_signal(
                 barrier, inc=1, device_id=(comp + dc, tile + dt), device_id_type=MESH
             )
+    own = pl.ds(HALO, OX)
+    quarter = lax.broadcasted_iota(jnp.int32, (OX, LANES), 1) // STRIP
+
+    def pack(kind):
+        low, high = KINDS[kind]
+        for side, column in ((0, BO - LANES), (1, 0)):
+            packed = jnp.zeros((OX, LANES), jnp.float32)
+            for f in range(high - low):
+                strip = x_ref[low + f, own, column:column + LANES]
+                shift = (STRIP * f + (STRIP if side == 0 else 0)) % LANES
+                if shift:
+                    strip = pltpu.roll(strip, shift, 1)
+                packed = jnp.where(quarter == f, strip, packed)
+            pack_ref[side, kind] = packed
+
+    lane = lax.broadcasted_iota(jnp.int32, (ROWS, LANES), 1)
+
+    def unpack(kind):
+        low, high = KINDS[kind]
+        for f in range(high - low):
+            left, right = side_ref[0, kind], side_ref[1, kind]
+            if f < 3:
+                left = pltpu.roll(left, LANES - STRIP - STRIP * f, 1)
+            if f > 0:
+                right = pltpu.roll(right, LANES - STRIP * f, 1)
+            x_ref[low + f, :, BO:WIDE] = jnp.where(
+                lane < STRIP, right, jnp.where(lane >= LANES - STRIP, left, 0.0)
+            )
+
+    x_ref[0:4, own, 0:BO] = fields_ref[...]
+    x_ref[4, own, 0:BO] = mask_ref[...].astype(jnp.float32)
+    pack(0)
+    pack(1)
     beside = [
         jnp.minimum(pos, 1) + jnp.minimum(size - 1 - pos, 1)
         for pos, size in ((comp, nc), (tile, nt))
@@ -159,8 +188,8 @@
 
     def halo_copy(phase, number):
         dc, dt = DIRECTIONS[number]
-        low, high = FIELDS_MASK if phase == 0 else FORCING
-        planes = pl.ds(low, high - low)
+        planes = pl.ds(0, 5) if phase == 0 else pl.ds(5, 4)
+        kinds = pl.ds(0, 2) if phase == 0 else pl.ds(2, 1)
         if dc == 0:
             src_rows, dst_rows = pl.ds(HALO, OX), pl.ds(HALO, OX)
         elif dc > 0:
@@ -170,12 +199,11 @@
         if dt == 0:
             src = x_ref.at[planes, src_rows, pl.ds(0, BO)]
             dst = x_ref.at[planes, dst_rows, pl.ds(0, BO)]
-        elif dt > 0:
-            src = x_ref.at[planes, src_rows, pl.ds(BO - LANES, LANES)]
-            dst = side_ref.at[0, planes, dst_rows, :]
         else:
-            src = x_ref.at[planes, src_rows, pl.ds(0, LANES)]
-            dst = side_ref.at[1, planes, dst_rows, :]
+            side = 0 if dt > 0 else 1
+            pack_rows = {0: pl.ds(0, OX), 1: pl.ds(OX - HALO, HALO), -1: pl.ds(0, HALO)}[dc]
+            src = pack_ref.at[side, kinds, pack_rows, :]
+            dst = side_ref.at[side, kinds, dst_rows, :]
         return pltpu.make_async_remote_copy(
             src_ref=src, dst_ref=dst,
             send_sem=halo_send.at[phase, number], recv_sem=halo_recv.at[phase, number],
@@ -199,11 +227,13 @@
                 halo_copy(phase, number).wait_recv()
 
     halo_start(0)
+    flux_all[tile] = flux_ref[...]
+    list_all[tile] = list_ref[...]
 
     mine = list_ref[...]
     row8 = lax.broadcasted_iota(jnp.int32, (8, LANES), 0)
-    own_block = (row8 == mine[0:1, :]).astype(jnp.bfloat16)
-    own_weight = (row8 == mine[3:4, :]).astype(jnp.bfloat16)
+    own_block = (row8 * nt + tile == mine[0:1, :]).astype(jnp.bfloat16)
+    own_weight = (row8 == mine[2:3, :]).astype(jnp.bfloat16)
     named = mm(own_block, own_weight, NT)
     ones = jnp.ones((16, BO), jnp.bfloat16)
     w_copy.wait()
@@ -222,11 +252,13 @@
 
     def count(source, carry):
         listing = list_all[source]
-        code = jnp.where(listing[1:2, :] == tile, listing[3:4, :] * OX + listing[2:3, :], -1)
+        row = listing[1:2, :] - tile * OX
+        here = jnp.logical_and(row >= 0, row < OX)
+        code = jnp.where(here, listing[2:3, :] * OX + row, -1)
         group = lax.broadcasted_iota(jnp.int32, (WTAB * OX, LANES), 0) == code
-        block = lax.broadcasted_iota(jnp.int32, (nt * ABLK, LANES), 0) == (
-            jnp.where(listing[0:1, :] >= 0, source * ABLK + listing[0:1, :], -1)
-        )
+        number = lax.broadcasted_iota(jnp.int32, (nt * ABLK, LANES), 0) - source * ABLK
+        number = jnp.where(jnp.logical_and(number >= 0, number < ABLK), number * nt + source, -2)
+        block = number == listing[0:1, :]
         group, block = group.astype(jnp.bfloat16), block.astype(jnp.bfloat16)
         counts[...] += mm(group, block, NT)
         counts_t[...] += mm(block, group, NT)
@@ -251,13 +283,13 @@
     acc = acc * forcing_rate
     for f in range(F):
         x_ref[5 + f, HALO:HALO + OX, 0:BO] = acc[f * OX:(f + 1) * OX]
+    pack(2)
     halo_start(1)
     halo_wait(0)
+    unpack(0)
+    unpack(1)
     halo_wait(1)
-
-    lane = lax.broadcasted_iota(jnp.int32, (ROWS, LANES), 1)
-    for k in range(9):
-        x_ref[k, :, BO:WIDE] = jnp.where(lane < LANES // 2, side_ref[1, k], side_ref[0, k])
+    unpack(2)
 
     done = 0
     while done < SUB:
@@ -289,12 +321,16 @@
     each_peer(lambda d: part_copy(d).start())
     part_in[tile] = part_out[tile]
     each_peer(lambda d: part_copy(d).wait())
-    sst_ref[...] = jnp.sum(part_in[...], axis=0) / denom[...]
+    regridded = jnp.sum(part_in[...], axis=0) / denom[...]
+    for k in range(BA // LANES):
+        sst_ref[pl.ds(k, ABLK, stride=BA // LANES), :] = (
+            regridded[:, k * LANES:(k + 1) * LANES]
+        )
 
 
 def body(nc, nt, columns, solver, warmth, weights, pairings, fields, indicator):
     renewed = jnp.dot(
-        solver, columns, precision=lax.Precision.HIGHEST, preferred_element_type=jnp.float32
+        solver, columns, precision=lax.Precision.HIGH, preferred_element_type=jnp.float32
     )
     air, moisture, wind_east, wind_north = (
         renewed[k * VERTICAL_LAYERS - 1] for k in (1, 2, 3, 4)
@@ -306,11 +342,8 @@
         speed * wind_east,
         speed * wind_north,
     ]).reshape(F, ABLK, BA)
-    listing = jnp.stack([
-        pairings[0] // nt, pairings[1] // OX, pairings[1] % OX, pairings[2]
-    ])
     listing = jnp.pad(
-        listing, ((0, 8 - 4), (0, LANES - listing.shape[1])), constant_values=-1
+        pairings, ((0, 8 - 3), (0, LANES - pairings.shape[1])), constant_values=-1
     )
     vmem = pl.BlockSpec(memory_space=pltpu.VMEM)
     f32, bf16 = jnp.float32, jnp.bfloat16
@@ -318,9 +351,9 @@
     stepped, regridded = pl.pallas_call(
         functools.partial(kernel, nc, nt),
         out_shape=(
-            jax.ShapeDtypeStruct((4, OX, BO), f32), jax.ShapeDtypeStruct((ABLK, BA), f32)
+            jax.ShapeDtypeStruct((4, OX, BO), f32), jax.ShapeDtypeStruct((ABLK * BA // LANES, LANES), f32)
         ),
-        in_specs=[vmem, vmem, pl.BlockSpec(memory_space=pl.ANY), vmem, vmem],
+        in_specs=[vmem, vmem, pl.BlockSpec(memory_space=pltpu.HBM), vmem, vmem],
         out_specs=(vmem, vmem),
         scratch_shapes=[
             pltpu.VMEM((nt, F, ABLK, BA), f32),
@@ -329,7 +362,8 @@
             pltpu.VMEM((WTAB, BA, BO), bf16),
             pltpu.VMEM((WTAB, BA, BO), bf16),
             pltpu.VMEM((9, ROWS, WIDE), f32),
-            pltpu.VMEM((2, 9, ROWS, LANES), f32),
+            pltpu.VMEM((2, 3, ROWS, LANES), f32),
+            pltpu.VMEM((2, 3, OX, LANES), f32),
             pltpu.VMEM((WTAB * OX, nt * ABLK), f32),
             pltpu.VMEM((nt * ABLK, WTAB * OX), f32),
             pltpu.VMEM((WTAB, 2 * F * OX, BA), bf16),
@@ -342,7 +376,7 @@
             dma((2, 8)), dma((2, 8)),
         ],
         compiler_params=pltpu.CompilerParams(
-            collective_id=0, has_side_effects=True, vmem_limit_bytes=48 * 1024 * 1024
+            collective_id=0, has_side_effects=True, vmem_limit_bytes=60 * 1024 * 1024
         ),
         name="coupling",
     )(flux, listing, weights, fields, indicator)

time: 44.6 us -> 42.3 us (0.948)
  Pallas kernels: 35.8 us -> 34.3 us
  matrix products: 2.42 us -> 1.75 us
    pallas_call x1, Pallas kernels: 35.8 us -> 34.3 us  [body(): pl.pallas_call(functools.partial(kernel, nc, nt), out_shape=(jax.ShapeDty...]
    unnamed x14 -> x8, local copies, waits for them, and re-layouts: 4.43 us -> 3 us
    pad x1, local copies, waits for them, and re-layouts: 0.01 us -> 1.4 us  [body(): jnp.pad(pairings, ((0, 8 - 3), (0, LANES - pairings.shape[1])), constant_...]
    select_n x2 -> x0, other arithmetic: 0.85 us -> none  [the longest x1 0.84 us: body(): pairings[0] // nt]
    another operation x1, other arithmetic: 0.01 us -> 0.8 us  [body(): jnp.stack([speed * (warmth - air), speed * (dewpoint_moisture_limit * war...]
    dot_general x1, matrix products: 2.42 us -> 1.75 us  [body(): jnp.dot(solver, columns, precision=lax.Precision.HIGH, preferred_element_...]
where the time goes in v2:
time: 42.3 us; the launch traced here: 42.1 us
  Pallas kernels  34.3 us (81%)
  local copies, waits for them, and re-layouts  4.42 us (10%)
  matrix products  1.75 us (4%)
  other arithmetic  0.9 us (2%)
  between operations  0.73 us (2%)
    pallas_call x1, Pallas kernels, body(): pl.pallas_call(functools.partial(kernel, nc, nt), out_shape=(jax.ShapeDty...  34.3 us
    unnamed x8, local copies, waits for them, and re-layouts  3 us
    dot_general x1, matrix products, body(): jnp.dot(solver, columns, precision=lax.Precision.HIGH, preferred_element_...  1.75 us
    pad x1, local copies, waits for them, and re-layouts, body(): jnp.pad(pairings, ((0, 8 - 3), (0, LANES - pairings.shape[1])), constant_...  1.4 us

profile of v2, /device:TPU:0, one launch (start us, length us, event | category | flops | bytes accessed | tf_op | source)
XLA Modules:
  0.0 42.1 jit_solution(13730726244428623702)
XLA Ops:
  0.6 0.0 copy-start
  0.6 1.4 %pad.4.list_ref = s32[8,128]{1,0:T(8,128)} pad(s32[3,64]{1,0:T(4,128)} %param.11, s32[]{:T(128)} %constant.3.clone.1), padding=0_5x0_64 | pad | bytes 4868 | tf_op jit(solution)/shard_map/jit(_pad)/pad | solution.py:345
  2.0 0.0 copy-done
  2.1 0.0 copy-start.2
  2.1 1.7 %fusion.1 = f32[192,2048]{1,0:T(8,128)S(1)} fusion(f32[192,192]{1,0:T(8,128)} %param.8, f32[192,2048]{1,0:T(8,128)S(1)} %copy-done), kind=kOutput, calls=%fused_computation.7 | convolution fusion | flops 452984832 | bytes 3293184 | tf_op jit(solution)/shard_map/dot_general | solution.py:332
  3.8 0.0 copy-start.1
  3.8 0.1 fusion
  3.9 0.0 copy-done.2
  4.0 0.8 %pad_maximum_fusion.flux_ref = f32[4,8,256]{2,1,0:T(8,128)} fusion(f32[1,8,256]{2,1,0:T(8,128)S(1)} %stack.18, f32[1,8,256]{2,1,0:T(8,128)S(1)} %stack.17, f32[1,8,256]{2,1,0:T(8,128)S(1)} %stack.16, f32[1,8,256]{2,1,0:T(8,128)S(1)} %stack.15), kind=kLoop, calls=%fused_computation | loop fusion | flops 24576 | bytes 65536 | tf_op jit(solution)/shard_map/stack | solution.py:339
  4.8 34.3 %coupling.1 = (f32[4,32,512]{2,1,0:T(8,128)}, f32[16,128]{1,0:T(8,128)}) custom-call(f32[4,8,256]{2,1,0:T(8,128)} %pad_maximum_fusion.flux_ref, s32[8,128]{1,0:T(8,128)} %pad.4.list_ref, f32[8,256,512]{2,1,0:T(8,128)} %w_hbm.1, f32[4,32,512]{2,1,0:T(8,128)} %fields_ref.1, s32[32,512]{1,0:T(8,128)} %mask_ref.1), custom_call_target="tpu_custom_call" | custom-call | tf_op jit(solution)/shard_map/coupling/pallas_call | solution.py:351
  39.1 0.0 copy-done.1
  39.1 1.7 %copy.12 = f32[4,32,512]{2,1,0:T(8,128)} copy(f32[4,32,512]{2,1,0:T(8,128)} %get-tuple-element.21) | data formatting | bytes 524288
  40.8 1.3 %copy.13 = f32[2048]{0:T(1024)} copy(f32[2048]{0:T(1024)} %bitcast.9) | data formatting | bytes 16384
  (5 shorter events, 0.0 us)
Async XLA Ops:
  0.6 1.4 %copy-start = (f32[192,2048]{1,0:T(8,128)S(1)}, f32[192,2048]{1,0:T(8,128)}, u32[]{:S(2)}) copy-start(f32[192,2048]{1,0:T(8,128)} %param.7) | copy-start | bytes 4718596
  2.1 1.9 %copy-start.2 = (f32[2048]{0:T(1024)S(1)}, f32[2048]{0:T(1024)}, u32[]{:S(2)}) copy-start(f32[2048]{0:T(1024)} %param.9) | copy-start | bytes 24580
  3.8 35.3 %copy-start.1 = (f32[192,2048]{1,0:T(8,128)}, f32[192,2048]{1,0:T(8,128)S(1)}, u32[]{:S(2)}) copy-start(f32[192,2048]{1,0:T(8,128)S(1)} %fusion.1) | copy-start | bytes 4718596

commit v3 on v2

--- a/solution.py
+++ b/solution.py
@@ -80,14 +80,16 @@
         before, here = here, after
 
 
-def kernel(nc, nt, flux_ref, list_ref, w_hbm, fields_ref, mask_ref, out_ref, sst_ref,
-           flux_all, list_all, w_ref, w_hi, w_lo, x_ref, side_ref, pack_ref, counts, counts_t, lhs,
+def kernel(nc, nt, columns_hbm, solver_ref, warmth_ref, pairs_ref, w_hbm, fields_ref, mask_ref,
+           out_ref, sst_ref, columns_ref, products, flux_ref, list_ref, columns_sem, flux_all, list_all, w_ref, w_hi, w_lo, x_ref, side_ref, pack_ref, counts, counts_t, lhs,
            z_ref, part_out, part_in, denom,
            w_sem, flux_send, flux_recv, list_send, list_recv, part_send, part_recv,
            halo_send, halo_recv):
     comp, tile = lax.axis_index("comp"), lax.axis_index("tile")
     w_copy = pltpu.make_async_copy(w_hbm, w_ref, w_sem)
     w_copy.start()
+    columns_copy = pltpu.make_async_copy(columns_hbm, columns_ref, columns_sem)
+    columns_copy.start()
 
     def inside(dc, dt):
         ok = None
@@ -150,6 +152,8 @@
                 lane < STRIP, right, jnp.where(lane >= LANES - STRIP, left, 0.0)
             )
 
+    list_ref[...] = jnp.full((8, LANES), -1, jnp.int32)
+    list_ref[0:3, 0:pairs_ref.shape[1]] = pairs_ref[...]
     x_ref[0:4, own, 0:BO] = fields_ref[...]
     x_ref[4, own, 0:BO] = mask_ref[...].astype(jnp.float32)
     pack(0)
@@ -184,7 +188,6 @@
         lax.fori_loop(1, nt, step, 0)
 
     each_peer(lambda d: list_copy(d).start())
-    each_peer(lambda d: flux_copy(d).start())
 
     def halo_copy(phase, number):
         dc, dt = DIRECTIONS[number]
@@ -227,6 +230,31 @@
                 halo_copy(phase, number).wait_recv()
 
     halo_start(0)
+
+    rows = jnp.concatenate(
+        [solver_ref[k * VERTICAL_LAYERS - 1:k * VERTICAL_LAYERS, :] for k in range(1, 5)], axis=0
+    )
+    rest = rows - rows.astype(jnp.bfloat16).astype(jnp.float32)
+    rows = jnp.concatenate([rows, rest, jnp.zeros((8, rows.shape[1]), jnp.float32)], axis=0)
+    rows = rows.astype(jnp.bfloat16)
+    columns_copy.wait()
+    high, low = split(columns_ref[...])
+    first, second = mm(rows, high, NN), mm(rows, low, NN)
+    mixed = first[0:4] + (first[4:8] + second[0:4])
+    for f in range(F):
+        for j in range(ABLK):
+            products[f, j:j + 1, :] = mixed[f:f + 1, j * BA:(j + 1) * BA]
+    pieces = BA // LANES
+    warmth = jnp.concatenate(
+        [warmth_ref[pl.ds(k, ABLK, stride=pieces), :] for k in range(pieces)], axis=1
+    )
+    air, moisture, wind_east, wind_north = (products[f] for f in range(F))
+    speed = transfer_constant * jnp.sqrt(wind_east * wind_east + wind_north * wind_north + 1.0)
+    flux_ref[0] = speed * (warmth - air)
+    flux_ref[1] = speed * (dewpoint_moisture_limit * warmth - moisture)
+    flux_ref[2] = speed * wind_east
+    flux_ref[3] = speed * wind_north
+    each_peer(lambda d: flux_copy(d).start())
     flux_all[tile] = flux_ref[...]
     list_all[tile] = list_ref[...]
 
@@ -332,20 +360,8 @@
     renewed = jnp.dot(
         solver, columns, precision=lax.Precision.HIGH, preferred_element_type=jnp.float32
     )
-    air, moisture, wind_east, wind_north = (
-        renewed[k * VERTICAL_LAYERS - 1] for k in (1, 2, 3, 4)
-    )
-    speed = transfer_constant * jnp.sqrt(wind_east * wind_east + wind_north * wind_north + 1.0)
-    flux = jnp.stack([
-        speed * (warmth - air),
-        speed * (dewpoint_moisture_limit * warmth - moisture),
-        speed * wind_east,
-        speed * wind_north,
-    ]).reshape(F, ABLK, BA)
-    listing = jnp.pad(
-        pairings, ((0, 8 - 3), (0, LANES - pairings.shape[1])), constant_values=-1
-    )
     vmem = pl.BlockSpec(memory_space=pltpu.VMEM)
+    hbm = pl.BlockSpec(memory_space=pltpu.HBM)
     f32, bf16 = jnp.float32, jnp.bfloat16
     dma = pltpu.SemaphoreType.DMA
     stepped, regridded = pl.pallas_call(
@@ -353,9 +369,14 @@
         out_shape=(
             jax.ShapeDtypeStruct((4, OX, BO), f32), jax.ShapeDtypeStruct((ABLK * BA // LANES, LANES), f32)
         ),
-        in_specs=[vmem, vmem, pl.BlockSpec(memory_space=pltpu.HBM), vmem, vmem],
+        in_specs=[hbm, vmem, vmem, vmem, hbm, vmem, vmem],
         out_specs=(vmem, vmem),
         scratch_shapes=[
+            pltpu.VMEM(columns.shape, f32),
+            pltpu.VMEM((F, ABLK, BA), f32),
+            pltpu.VMEM((F, ABLK, BA), f32),
+            pltpu.VMEM((8, LANES), jnp.int32),
+            dma,
             pltpu.VMEM((nt, F, ABLK, BA), f32),
             pltpu.VMEM((nt, 8, LANES), jnp.int32),
             pltpu.VMEM((WTAB, BA, BO), f32),
@@ -379,7 +400,7 @@
             collective_id=0, has_side_effects=True, vmem_limit_bytes=60 * 1024 * 1024
         ),
         name="coupling",
-    )(flux, listing, weights, fields, indicator)
+    )(columns, solver, warmth.reshape(-1, LANES), pairings, weights, fields, indicator)
     return renewed, stepped, regridded.reshape(-1)
 
 

time: 42.3 us -> 39.2 us (0.927)
  local copies, waits for them, and re-layouts: 4.42 us -> 1.32 us
  other arithmetic: 0.9 us -> 0 us
  Pallas kernels: 34.3 us -> 35.1 us
    unnamed x8 -> x10, local copies, waits for them, and re-layouts: 3 us -> 1.32 us
    pad x1 -> x0, local copies, waits for them, and re-layouts: 1.4 us -> none  [body(): jnp.pad(pairings, ((0, 8 - 3), (0, LANES - pairings.shape[1])), constant_...]
    pallas_call x1, Pallas kernels: 34.3 us -> 35.1 us  [body(): pl.pallas_call(functools.partial(kernel, nc, nt), out_shape=(jax.ShapeDty...]
    another operation x1 -> x0, other arithmetic: 0.8 us -> none  [body(): jnp.stack([speed * (warmth - air), speed * (dewpoint_moisture_limit * war...]
where the time goes in v3:
time: 39.2 us; the launch traced here: 39.1 us
  Pallas kernels  35.1 us (90%)
  matrix products  1.97 us (5%)
  local copies, waits for them, and re-layouts  1.32 us (3%)
  between operations  0.69 us (2%)
    pallas_call x1, Pallas kernels, body(): pl.pallas_call(functools.partial(kernel, nc, nt), out_shape=(jax.ShapeDty...  35.1 us
    dot_general x1, matrix products, body(): jnp.dot(solver, columns, precision=lax.Precision.HIGH, preferred_element_...  1.97 us
    unnamed x10, local copies, waits for them, and re-layouts  1.32 us

profile of v3, /device:TPU:0, one launch (start us, length us, event | category | flops | bytes accessed | tf_op | source)
XLA Modules:
  0.0 39.1 jit_solution(7851648149144048873)
XLA Ops:
  0.6 0.0 copy-start
  0.6 0.0 copy-start.1
  0.7 35.1 %coupling.1 = (f32[4,32,512]{2,1,0:T(8,128)}, f32[16,128]{1,0:T(8,128)}) custom-call(f32[192,2048]{1,0:T(8,128)} %columns_hbm.1, f32[192,192]{1,0:T(8,128)} %solver_ref.1, f32[16,128]{1,0:T(8,128)} %bitcast.4, s32[3,64]{1,0:T(4,128)} %pairs_ref.1, f32[8,256,512]{2,1,0:T(8,128)} %w_hbm.1, f32[4,32,512]{2,1,0:T(8,128)} %fields_ref.1, s32[32,512]{1,0:T(8,128)} %mask_ref.1), custom_call_target="tpu_custom_call" | custom-call | tf_op jit(solution)/shard_map/coupling/pallas_call | solution.py:367
  35.8 0.0 copy-done
  35.8 0.0 copy-done.1
  35.8 0.0 copy-start.2
  35.8 0.0 copy-start.3
  35.8 2.0 %fusion = f32[192,2048]{1,0:T(8,128)} fusion(f32[192,192]{1,0:T(8,128)S(1)} %copy-done.1, f32[192,2048]{1,0:T(8,128)S(1)} %copy-done), kind=kOutput, calls=%fused_computation | convolution fusion | flops 452984832 | bytes 3293184 | tf_op jit(solution)/shard_map/dot_general | solution.py:360
  37.8 0.0 copy-done.2
  37.8 0.7 %copy.12 = f32[4,32,512]{2,1,0:T(8,128)} copy(f32[4,32,512]{2,1,0:T(8,128)S(1)} %copy-done.2) | data formatting | bytes 524288
  38.5 0.0 copy-done.3
  38.5 0.6 %copy.13 = f32[2048]{0:T(1024)} copy(f32[2048]{0:T(1024)S(1)} %bitcast.5) | data formatting | bytes 16384
Async XLA Ops:
  0.6 35.2 %copy-start = (f32[192,2048]{1,0:T(8,128)S(1)}, f32[192,2048]{1,0:T(8,128)}, u32[]{:S(2)}) copy-start(f32[192,2048]{1,0:T(8,128)} %columns_hbm.1) | copy-start | bytes 4718596
  0.6 35.2 %copy-start.1 = (f32[192,192]{1,0:T(8,128)S(1)}, f32[192,192]{1,0:T(8,128)}, u32[]{:S(2)}) copy-start(f32[192,192]{1,0:T(8,128)} %solver_ref.1) | copy-start | bytes 442372
  35.8 2.0 %copy-start.2 = (f32[4,32,512]{2,1,0:T(8,128)S(1)}, f32[4,32,512]{2,1,0:T(8,128)}, u32[]{:S(2)}) copy-start(f32[4,32,512]{2,1,0:T(8,128)} %get-tuple-element.11) | copy-start | bytes 786436
  35.8 2.7 %copy-start.3 = (f32[16,128]{1,0:T(8,128)S(1)}, f32[16,128]{1,0:T(8,128)}, u32[]{:S(2)}) copy-start(f32[16,128]{1,0:T(8,128)} %get-tuple-element.6) | copy-start | bytes 24580

commit v4 on v3

--- a/solution.py
+++ b/solution.py
@@ -213,8 +213,10 @@
             device_id=(comp + dc, tile + dt), device_id_type=MESH,
         )
 
-    def halo_start(phase):
-        for number, (dc, dt) in enumerate(DIRECTIONS):
+    def halo_start(phase, numbers=range(8)):
+        for number in numbers:
+            dc, dt = DIRECTIONS[number]
+
             @pl.when(inside(dc, dt))
             def _():
                 halo_copy(phase, number).start()
@@ -311,8 +313,9 @@
     acc = acc * forcing_rate
     for f in range(F):
         x_ref[5 + f, HALO:HALO + OX, 0:BO] = acc[f * OX:(f + 1) * OX]
+    halo_start(1, range(2))
     pack(2)
-    halo_start(1)
+    halo_start(1, range(2, 8))
     halo_wait(0)
     unpack(0)
     unpack(1)
@@ -336,7 +339,6 @@
         lax.fori_loop(0, upto - done, substep, 0)
         done = upto
 
-    out_ref[...] = x_ref[0:4, HALO:HALO + OX, 0:BO]
     high, low = split(x_ref[3, HALO:HALO + OX, 0:BO])
     both = jnp.concatenate([high, low], axis=0)
     for w in range(WTAB):
@@ -347,6 +349,7 @@
     partial = mm(count_bw, high, NN) + mm(count_bw, low, NN)
     part_out[...] = partial.reshape(nt, ABLK, BA)
     each_peer(lambda d: part_copy(d).start())
+    out_ref[...] = x_ref[0:4, HALO:HALO + OX, 0:BO]
     part_in[tile] = part_out[tile]
     each_peer(lambda d: part_copy(d).wait())
     regridded = jnp.sum(part_in[...], axis=0) / denom[...]

time: 39.2 us -> 39.2 us (level)
  no operation moved by 1% of the time
where the time goes in v4:
time: 39.2 us; the launch traced here: 39 us
  Pallas kernels  35.1 us (90%)
  matrix products  1.97 us (5%)
  local copies, waits for them, and re-layouts  1.32 us (3%)
  between operations  0.69 us (2%)
    pallas_call x1, Pallas kernels, body(): pl.pallas_call(functools.partial(kernel, nc, nt), out_shape=(jax.ShapeDty...  35.1 us
    dot_general x1, matrix products, body(): jnp.dot(solver, columns, precision=lax.Precision.HIGH, preferred_element_...  1.97 us
    unnamed x10, local copies, waits for them, and re-layouts  1.32 us

profile of v4, /device:TPU:0, one launch (start us, length us, event | category | flops | bytes accessed | tf_op | source)
XLA Modules:
  0.0 39.0 jit_solution(13791328322891294654)
XLA Ops:
  0.6 0.0 copy-start
  0.6 0.0 copy-start.1
  0.7 35.1 %coupling.1 = (f32[4,32,512]{2,1,0:T(8,128)}, f32[16,128]{1,0:T(8,128)}) custom-call(f32[192,2048]{1,0:T(8,128)} %columns_hbm.1, f32[192,192]{1,0:T(8,128)} %solver_ref.1, f32[16,128]{1,0:T(8,128)} %bitcast.4, s32[3,64]{1,0:T(4,128)} %pairs_ref.1, f32[8,256,512]{2,1,0:T(8,128)} %w_hbm.1, f32[4,32,512]{2,1,0:T(8,128)} %fields_ref.1, s32[32,512]{1,0:T(8,128)} %mask_ref.1), custom_call_target="tpu_custom_call" | custom-call | tf_op jit(solution)/shard_map/coupling/pallas_call | solution.py:370
  35.7 0.0 copy-done
  35.7 0.0 copy-done.1
  35.7 0.0 copy-start.2
  35.7 0.0 copy-start.3
  35.8 2.0 %fusion = f32[192,2048]{1,0:T(8,128)} fusion(f32[192,192]{1,0:T(8,128)S(1)} %copy-done.1, f32[192,2048]{1,0:T(8,128)S(1)} %copy-done), kind=kOutput, calls=%fused_computation | convolution fusion | flops 452984832 | bytes 3293184 | tf_op jit(solution)/shard_map/dot_general | solution.py:363
  37.7 0.0 copy-done.2
  37.7 0.7 %copy.12 = f32[4,32,512]{2,1,0:T(8,128)} copy(f32[4,32,512]{2,1,0:T(8,128)S(1)} %copy-done.2) | data formatting | bytes 524288
  38.4 0.0 copy-done.3
  38.4 0.6 %copy.13 = f32[2048]{0:T(1024)} copy(f32[2048]{0:T(1024)S(1)} %bitcast.5) | data formatting | bytes 16384
Async XLA Ops:
  0.6 35.1 %copy-start = (f32[192,2048]{1,0:T(8,128)S(1)}, f32[192,2048]{1,0:T(8,128)}, u32[]{:S(2)}) copy-start(f32[192,2048]{1,0:T(8,128)} %columns_hbm.1) | copy-start | bytes 4718596
  0.6 35.1 %copy-start.1 = (f32[192,192]{1,0:T(8,128)S(1)}, f32[192,192]{1,0:T(8,128)}, u32[]{:S(2)}) copy-start(f32[192,192]{1,0:T(8,128)} %solver_ref.1) | copy-start | bytes 442372
  35.7 2.0 %copy-start.2 = (f32[4,32,512]{2,1,0:T(8,128)S(1)}, f32[4,32,512]{2,1,0:T(8,128)}, u32[]{:S(2)}) copy-start(f32[4,32,512]{2,1,0:T(8,128)} %get-tuple-element.11) | copy-start | bytes 786436
  35.7 2.7 %copy-start.3 = (f32[16,128]{1,0:T(8,128)S(1)}, f32[16,128]{1,0:T(8,128)}, u32[]{:S(2)}) copy-start(f32[16,128]{1,0:T(8,128)} %get-tuple-element.6) | copy-start | bytes 24580
